TPU v7x, 256 devices: a whole 4x4x8 slice. The times are simulated.
256 devices in a mesh: seq: 32 (over x, z), grp: 8 (over y, core).
Axes of the slice: x: 4, y: 4, z: 8, core: 2. Of those that a mesh axis runs over, the one named last changes fastest.
Arguments:
- queries: bfloat16 [32768, 4096], P(('grp', 'seq')), parts along dimension 0, may hold values from -8.5 to 8.5
- keys: bfloat16 [32768, 512], P(('grp', 'seq')), parts along dimension 0, may hold values from -6 to 6
- values: bfloat16 [32768, 512], P(('grp', 'seq')), parts along dimension 0, may hold values from -6 to 6
- out_grad: bfloat16 [32768, 4096], P(('grp', 'seq')), parts along dimension 0, may hold values from -6 to 6
- doc_lengths: int32 [64], P('grp'), parts along dimension 0, may hold values from 1 to 1024, 4096 in all
- span_order: int32 [512], P('grp'), parts along dimension 0, may hold values from 0 to 63, each once
Outputs:
- attended: bfloat16 [32768, 4096], P(('grp', 'seq')), parts along dimension 0
- grad_q: bfloat16 [32768, 4096], P(('grp', 'seq')), parts along dimension 0
- grad_k: bfloat16 [32768, 512], P(('grp', 'seq')), parts along dimension 0
- grad_v: bfloat16 [32768, 512], P(('grp', 'seq')), parts along dimension 0
There are 8 independent parts, one for each index of `grp`. A program takes and returns all parts, laid end to end along the dimension named above; each array names one. Nothing has to cross between parts.
Inputs may be any that keep to these rules, and one draw needn't show every extreme that they name: `doc_lengths`: the lengths sum to 4096; the longest is exactly 1024. `span_order`: each span number appears once.
All inputs are finite; a program needn't handle non-finite values.
Results may differ from a plain program's by a relative error of at most 0.015.
Values may be sent and summed in bfloat16 or wider, within the bound.
A program may use at most 64 MiB of HBM per device.

v0:
```python
import jax
import jax.numpy as jnp
from jax import lax
from jax.sharding import PartitionSpec as P

QUERY_HEADS = 32
KEY_VALUE_HEADS = 4
HEAD_SIZE = 128
BLK = 512


neg_big = -1e30


def doc_index(doc_lengths, packed_length):
    starts = jnp.cumsum(doc_lengths) - doc_lengths
    places = jnp.arange(packed_length, dtype=jnp.int32)
    return jnp.sum((places[:, None] >= starts[None, 1:]).astype(jnp.int32), axis=1)


def is_live(docs, row_blk, col_blk):
    return docs[col_blk * BLK + BLK - 1] >= docs[row_blk * BLK]


def block_scores(q_block, k_place, docs, row_blk, col_blk, scale):
    k_block = lax.dynamic_slice_in_dim(k_place, col_blk * BLK, BLK, 0)
    scores = jnp.dot(q_block, k_block.T, preferred_element_type=jnp.float32) * scale
    offsets = jnp.arange(BLK, dtype=jnp.int32)
    q_docs = lax.dynamic_slice_in_dim(docs, row_blk * BLK, BLK, 0)
    k_docs = lax.dynamic_slice_in_dim(docs, col_blk * BLK, BLK, 0)
    visible = ((col_blk * BLK + offsets)[None, :] <= (row_blk * BLK + offsets)[:, None]) & (
        k_docs[None, :] == q_docs[:, None]
    )
    return (jnp.where(visible, scores, neg_big), visible)


def block_probs(q_block, k_place, docs, row_blk, col_blk, scale, top, total):
    scores, visible = block_scores(q_block, k_place, docs, row_blk, col_blk, scale)
    return jnp.where(visible, jnp.exp(scores - top[:, None]) / total[:, None], 0.0)


def forward_head(q_place, k_place, v_place, docs, scale):
    blocks = q_place.shape[0] // BLK

    def forward_one_block(row_blk):
        q_block = lax.dynamic_slice_in_dim(q_place, row_blk * BLK, BLK, 0)

        def stats(col_blk, carry):

            def stats_live(state):
                scores, visible = block_scores(q_block, k_place, docs, row_blk, col_blk, scale)
                new_top = jnp.maximum(state[0], jnp.max(scores, axis=1))
                weights = jnp.where(visible, jnp.exp(scores - new_top[:, None]), 0.0)
                return (new_top, state[1] * jnp.exp(state[0] - new_top) + jnp.sum(weights, axis=1))

            return lax.cond(is_live(docs, row_blk, col_blk), stats_live, lambda state: state, carry)

        start = (jnp.full((BLK,), neg_big, jnp.float32), jnp.zeros((BLK,), jnp.float32))
        top, total = lax.fori_loop(0, row_blk + 1, stats, start)

        def add_values(col_blk, accum):

            def add_live(running):
                probs = block_probs(q_block, k_place, docs, row_blk, col_blk, scale, top, total)
                v_block = lax.dynamic_slice_in_dim(v_place, col_blk * BLK, BLK, 0)
                return running + jnp.dot(
                    probs.astype(jnp.bfloat16), v_block, preferred_element_type=jnp.float32
                )

            return lax.cond(
                is_live(docs, row_blk, col_blk), add_live, lambda running: running, accum
            )

        accum = lax.fori_loop(
            0, row_blk + 1, add_values, jnp.zeros((BLK, q_place.shape[1]), jnp.float32)
        )
        return (accum.astype(jnp.bfloat16), top, total)

    outputs, tops, totals = lax.map(forward_one_block, jnp.arange(blocks, dtype=jnp.int32))
    return (outputs.reshape(q_place.shape[0], q_place.shape[1]), tops, totals)


def backward_head(q_place, k_place, v_place, g_place, o_place, tops, totals, docs, scale):
    blocks = q_place.shape[0] // BLK
    width = q_place.shape[1]

    def backward_one_block(carry, row_blk):
        q_block = lax.dynamic_slice_in_dim(q_place, row_blk * BLK, BLK, 0)
        g_block = lax.dynamic_slice_in_dim(g_place, row_blk * BLK, BLK, 0)
        o_block = lax.dynamic_slice_in_dim(o_place, row_blk * BLK, BLK, 0)
        top = tops[row_blk]
        total = totals[row_blk]
        delta = jnp.sum(o_block.astype(jnp.float32) * g_block.astype(jnp.float32), axis=1)

        def step(col_blk, state):

            def step_live(inner):
                q_grad, k_grad, v_grad = inner
                probs = block_probs(q_block, k_place, docs, row_blk, col_blk, scale, top, total)
                rounded = probs.astype(jnp.bfloat16)
                k_block = lax.dynamic_slice_in_dim(k_place, col_blk * BLK, BLK, 0)
                v_block = lax.dynamic_slice_in_dim(v_place, col_blk * BLK, BLK, 0)
                pressure = jnp.dot(g_block, v_block.T, preferred_element_type=jnp.float32)
                slopes = (probs * (pressure - delta[:, None])).astype(jnp.bfloat16)
                q_grad = q_grad + jnp.dot(slopes, k_block, preferred_element_type=jnp.float32)
                k_rows = lax.dynamic_slice_in_dim(k_grad, col_blk * BLK, BLK, 0) + jnp.einsum(
                    "qk,qd->kd", slopes, q_block, preferred_element_type=jnp.float32
                )
                v_rows = lax.dynamic_slice_in_dim(v_grad, col_blk * BLK, BLK, 0) + jnp.einsum(
                    "qk,qd->kd", rounded, g_block, preferred_element_type=jnp.float32
                )
                k_grad = lax.dynamic_update_slice_in_dim(k_grad, k_rows, col_blk * BLK, 0)
                v_grad = lax.dynamic_update_slice_in_dim(v_grad, v_rows, col_blk * BLK, 0)
                return (q_grad, k_grad, v_grad)

            return lax.cond(is_live(docs, row_blk, col_blk), step_live, lambda inner: inner, state)

        start = (jnp.zeros((BLK, width), jnp.float32), carry[0], carry[1])
        q_grad, k_grad, v_grad = lax.fori_loop(0, row_blk + 1, step, start)
        return ((k_grad, v_grad), (q_grad * scale).astype(jnp.bfloat16))

    empty = jnp.zeros(q_place.shape, jnp.float32)
    (k_grad, v_grad), q_grads = lax.scan(
        backward_one_block, (empty, empty), jnp.arange(blocks, dtype=jnp.int32)
    )
    return (q_grads.reshape(q_place.shape[0], width), k_grad * scale, v_grad)


def on_device(queries, keys, values, out_grad, doc_lengths, span_order):
    parts = lax.axis_size("seq")
    token_rows = queries.shape[0]
    packed_length = token_rows * parts
    head_group = QUERY_HEADS // KEY_VALUE_HEADS
    scale = HEAD_SIZE ** (-0.5)

    def widen(block_tile):
        spread_heads = jnp.broadcast_to(
            block_tile.reshape(token_rows, KEY_VALUE_HEADS, 1, HEAD_SIZE),
            (token_rows, KEY_VALUE_HEADS, head_group, HEAD_SIZE),
        )
        return spread_heads.reshape(token_rows, QUERY_HEADS * HEAD_SIZE)

    k_wide = widen(keys)
    v_wide = widen(values)
    q_heads, k_heads, v_heads, g_heads = (
        lax.all_to_all(queries, "seq", split_axis=1, concat_axis=0, tiled=True),
        lax.all_to_all(k_wide, "seq", split_axis=1, concat_axis=0, tiled=True),
        lax.all_to_all(v_wide, "seq", split_axis=1, concat_axis=0, tiled=True),
        lax.all_to_all(out_grad, "seq", split_axis=1, concat_axis=0, tiled=True),
    )
    spans = span_order.shape[0]
    half = packed_length // spans
    inverse = jnp.argsort(span_order)

    def into_placement(block_tile):
        return block_tile.reshape(spans, half, block_tile.shape[1])[inverse].reshape(
            packed_length, block_tile.shape[1]
        )

    def into_layout(block_tile):
        return block_tile.reshape(spans, half, block_tile.shape[1])[span_order].reshape(
            packed_length, block_tile.shape[1]
        )

    docs = doc_index(doc_lengths, packed_length)
    q_place = into_placement(q_heads)
    k_place = into_placement(k_heads)
    v_place = into_placement(v_heads)
    forwards = [forward_head(q_place, k_place, v_place, docs, scale)]
    attended_place = jnp.concatenate([result[0] for result in forwards], axis=1)
    attended_lay = into_layout(attended_place)
    g_place = into_placement(g_heads)
    backwards = [
        backward_head(
            q_place,
            k_place,
            v_place,
            g_place,
            forwards[0][0],
            forwards[0][1],
            forwards[0][2],
            docs,
            scale,
        )
    ]
    q_grad_lay = into_layout(jnp.concatenate([result[0] for result in backwards], axis=1))
    k_part_lay = into_layout(jnp.concatenate([result[1] for result in backwards], axis=1))
    v_part_lay = into_layout(jnp.concatenate([result[2] for result in backwards], axis=1))
    attended, grad_q = (
        lax.all_to_all(attended_lay, "seq", split_axis=0, concat_axis=1, tiled=True),
        lax.all_to_all(q_grad_lay, "seq", split_axis=0, concat_axis=1, tiled=True),
    )
    k_back, v_back = (
        lax.all_to_all(
            k_part_lay.astype(jnp.bfloat16), "seq", split_axis=0, concat_axis=1, tiled=True
        ).astype(k_part_lay.dtype),
        lax.all_to_all(
            v_part_lay.astype(jnp.bfloat16), "seq", split_axis=0, concat_axis=1, tiled=True
        ).astype(v_part_lay.dtype),
    )

    def narrow(block_tile):
        group_summed = jnp.sum(
            block_tile.reshape(token_rows, KEY_VALUE_HEADS, head_group, HEAD_SIZE), axis=2
        )
        return group_summed.reshape(token_rows, KEY_VALUE_HEADS * HEAD_SIZE).astype(jnp.bfloat16)

    return (attended, grad_q, narrow(k_back), narrow(v_back))


def solution(mesh):
    placed = (
        P(("grp", "seq"), None),
        P(("grp", "seq"), None),
        P(("grp", "seq"), None),
        P(("grp", "seq"), None),
        P("grp"),
        P("grp"),
    )
    return jax.shard_map(
        on_device,
        mesh=mesh,
        in_specs=placed,
        out_specs=(
            P(("grp", "seq"), None),
            P(("grp", "seq"), None),
            P(("grp", "seq"), None),
            P(("grp", "seq"), None),
        ),
        check_vma=False,
    )
```

profile of v0, /device:TPU:8, one launch (start us, length us, event | category | flops | bytes accessed | tf_op | source)
XLA Modules:
  0.0 709.4 jit_solution(11412684361091045754)
XLA Ops:
  2.9 11.3 %all-to-all-start = ((bf16[128,32,128]{0,2,1:T(8,128)(2,1)}), bf16[128,32,128]{0,2,1:T(8,128)(2,1)S(1)}, u32[]{:S(2)}, u32[]{:S(2)}) async-start(bf16[128,32,128]{0,2,1:T(8,128)(2,1)} %bitcast.15), calls=%async_computation | async-start | bytes 2097152 | tf_op jit(solution)/shard_map/all_to_all | solution.py:146
  14.3 28.6 %all-to-all-done = bf16[128,32,128]{0,2,1:T(8,128)(2,1)S(1)} async-done(((bf16[128,32,128]{0,2,1:T(8,128)(2,1)}), bf16[128,32,128]{0,2,1:T(8,128)(2,1)S(1)}, u32[]{:S(2)}, u32[]{:S(2)}) %all-to-all-start) | async-done | bytes 1048608 | tf_op jit(solution)/shard_map/all_to_all | solution.py:146
  49.4 28.2 %all-to-all-done.1 = bf16[128,32,128]{2,0,1:T(8,128)(2,1)S(1)} async-done(((bf16[128,32,128]{2,0,1:T(8,128)(2,1)}), bf16[128,32,128]{2,0,1:T(8,128)(2,1)S(1)}, u32[]{:S(2)}, u32[]{:S(2)}) %all-to-all-start.1) | async-done | bytes 1048608 | tf_op jit(solution)/shard_map/all_to_all | solution.py:147
  93.3 18.9 %all-to-all-done.2 = bf16[128,32,128]{2,0,1:T(8,128)(2,1)S(1)} async-done(((bf16[128,32,128]{2,0,1:T(8,128)(2,1)}), bf16[128,32,128]{2,0,1:T(8,128)(2,1)S(1)}, u32[]{:S(2)}, u32[]{:S(2)}) %all-to-all-start.2) | async-done | bytes 1048608 | tf_op jit(solution)/shard_map/all_to_all | solution.py:148
  119.1 215.7 %while.125 = (s32[]{:T(128)}, bf16[8,512,128]{2,1,0:T(8,128)(2,1)}, f32[8,512]{1,0:T(8,128)S(1)}, f32[8,512]{1,0:T(8,128)S(1)}, s32[8]{0:T(128)S(1)}, /*index=5*...) while((s32[]{:T(128)}, bf16[8,512,128]{2,1,0:T(8,128)(2,1)}, ...), condition=%wide.region_14.15_spmd, body=%wide.region_3.14_spmd.sunk | while | flops 206965792 | bytes 4289429 | solution.py:79
  150.7 8.5 %while.128 = (s32[]{:T(128)}, f32[512]{0:T(512)S(1)}, f32[512]{0:T(512)S(1)}, s32[]{:T(128)}, s32[4096]{0:T(1024)S(1)}, /*index=5*/s32[1]{0:T(128)}, s32[]{:T(12...) while((s32[]{:T(128)}, f32[512]{0:T(512)S(1)}, ...), condition=%wide.region_9.9_spmd, body=%wide.region_4.8_spmd.sunk | while | flops 70256656 | bytes 2415017 | solution.py:59
  159.2 8.8 %while.129 = (s32[]{:T(128)}, f32[512,128]{1,0:T(8,128)S(1)}, s32[]{:T(128)}, s32[4096]{0:T(1024)S(1)}, s32[1]{0:T(128)}, /*index=5*/s32[]{:T(128)}, bf16[4096,1...) while((s32[]{:T(128)}, f32[512,128]{1,0:T(8,128)S(1)}, ...), condition=%wide.region_13.13_spmd, body=%wide.region_10.12_spmd.sunk | while | flops 136643584 | bytes 943525 | solution.py:74
  172.0 11.8 %while.128 = (s32[]{:T(128)}, f32[512]{0:T(512)S(1)}, f32[512]{0:T(512)S(1)}, s32[]{:T(128)}, s32[4096]{0:T(1024)S(1)}, /*index=5*/s32[1]{0:T(128)}, s32[]{:T(12...) while((s32[]{:T(128)}, f32[512]{0:T(512)S(1)}, ...), condition=%wide.region_9.9_spmd, body=%wide.region_4.8_spmd.sunk | while | flops 70256656 | bytes 2415017 | solution.py:59
  183.8 12.2 %while.129 = (s32[]{:T(128)}, f32[512,128]{1,0:T(8,128)S(1)}, s32[]{:T(128)}, s32[4096]{0:T(1024)S(1)}, s32[1]{0:T(128)}, /*index=5*/s32[]{:T(128)}, bf16[4096,1...) while((s32[]{:T(128)}, f32[512,128]{1,0:T(8,128)S(1)}, ...), condition=%wide.region_13.13_spmd, body=%wide.region_10.12_spmd.sunk | while | flops 136643584 | bytes 943525 | solution.py:74
  200.0 12.3 %while.128 = (s32[]{:T(128)}, f32[512]{0:T(512)S(1)}, f32[512]{0:T(512)S(1)}, s32[]{:T(128)}, s32[4096]{0:T(1024)S(1)}, /*index=5*/s32[1]{0:T(128)}, s32[]{:T(12...) while((s32[]{:T(128)}, f32[512]{0:T(512)S(1)}, ...), condition=%wide.region_9.9_spmd, body=%wide.region_4.8_spmd.sunk | while | flops 70256656 | bytes 2415017 | solution.py:59
  212.3 12.5 %while.129 = (s32[]{:T(128)}, f32[512,128]{1,0:T(8,128)S(1)}, s32[]{:T(128)}, s32[4096]{0:T(1024)S(1)}, s32[1]{0:T(128)}, /*index=5*/s32[]{:T(128)}, bf16[4096,1...) while((s32[]{:T(128)}, f32[512,128]{1,0:T(8,128)S(1)}, ...), condition=%wide.region_13.13_spmd, body=%wide.region_10.12_spmd.sunk | while | flops 136643584 | bytes 943525 | solution.py:74
  228.9 14.1 %while.128 = (s32[]{:T(128)}, f32[512]{0:T(512)S(1)}, f32[512]{0:T(512)S(1)}, s32[]{:T(128)}, s32[4096]{0:T(1024)S(1)}, /*index=5*/s32[1]{0:T(128)}, s32[]{:T(12...) while((s32[]{:T(128)}, f32[512]{0:T(512)S(1)}, ...), condition=%wide.region_9.9_spmd, body=%wide.region_4.8_spmd.sunk | while | flops 70256656 | bytes 2415017 | solution.py:59
  243.1 14.4 %while.129 = (s32[]{:T(128)}, f32[512,128]{1,0:T(8,128)S(1)}, s32[]{:T(128)}, s32[4096]{0:T(1024)S(1)}, s32[1]{0:T(128)}, /*index=5*/s32[]{:T(128)}, bf16[4096,1...) while((s32[]{:T(128)}, f32[512,128]{1,0:T(8,128)S(1)}, ...), condition=%wide.region_13.13_spmd, body=%wide.region_10.12_spmd.sunk | while | flops 136643584 | bytes 943525 | solution.py:74
  261.5 16.0 %while.128 = (s32[]{:T(128)}, f32[512]{0:T(512)S(1)}, f32[512]{0:T(512)S(1)}, s32[]{:T(128)}, s32[4096]{0:T(1024)S(1)}, /*index=5*/s32[1]{0:T(128)}, s32[]{:T(12...) while((s32[]{:T(128)}, f32[512]{0:T(512)S(1)}, ...), condition=%wide.region_9.9_spmd, body=%wide.region_4.8_spmd.sunk | while | flops 70256656 | bytes 2415017 | solution.py:59
  277.6 16.3 %while.129 = (s32[]{:T(128)}, f32[512,128]{1,0:T(8,128)S(1)}, s32[]{:T(128)}, s32[4096]{0:T(1024)S(1)}, s32[1]{0:T(128)}, /*index=5*/s32[]{:T(128)}, bf16[4096,1...) while((s32[]{:T(128)}, f32[512,128]{1,0:T(8,128)S(1)}, ...), condition=%wide.region_13.13_spmd, body=%wide.region_10.12_spmd.sunk | while | flops 136643584 | bytes 943525 | solution.py:74
  297.9 17.9 %while.128 = (s32[]{:T(128)}, f32[512]{0:T(512)S(1)}, f32[512]{0:T(512)S(1)}, s32[]{:T(128)}, s32[4096]{0:T(1024)S(1)}, /*index=5*/s32[1]{0:T(128)}, s32[]{:T(12...) while((s32[]{:T(128)}, f32[512]{0:T(512)S(1)}, ...), condition=%wide.region_9.9_spmd, body=%wide.region_4.8_spmd.sunk | while | flops 70256656 | bytes 2415017 | solution.py:59
  315.9 18.2 %while.129 = (s32[]{:T(128)}, f32[512,128]{1,0:T(8,128)S(1)}, s32[]{:T(128)}, s32[4096]{0:T(1024)S(1)}, s32[1]{0:T(128)}, /*index=5*/s32[]{:T(128)}, bf16[4096,1...) while((s32[]{:T(128)}, f32[512,128]{1,0:T(8,128)S(1)}, ...), condition=%wide.region_13.13_spmd, body=%wide.region_10.12_spmd.sunk | while | flops 136643584 | bytes 943525 | solution.py:74
  341.6 237.8 %while.127 = (s32[]{:T(128)}, f32[4096,128]{1,0:T(8,128)S(1)}, f32[4096,128]{1,0:T(8,128)}, bf16[8,512,128]{2,1,0:T(8,128)(2,1)}, s32[8]{0:T(128)S(1)}, /*index=...) while((s32[]{:T(128)}, f32[4096,128]{1,0:T(8,128)S(1)}, ...), condition=%wide.region_21.22_spmd, body=%wide.region_15.21_spmd.sunk | while | flops 339280384 | bytes 8689194 | solution.py:123
  348.0 8.8 %while.130 = (s32[]{:T(128)}, f32[512,128]{1,0:T(8,128)S(1)}, f32[4096,128]{1,0:T(8,128)S(1)}, f32[4096,128]{1,0:T(8,128)}, s32[]{:T(128)}, /*index=5*/s32[4096]...) while((s32[]{:T(128)}, f32[512,128]{1,0:T(8,128)S(1)}, ...), condition=%wide.region_20.20_spmd, body=%wide.region_17.19_spmd.sunk | while | flops 338887680 | bytes 7236137 | solution.py:119
  350.0 6.9 conditional.6
  364.1 17.7 %while.130 = (s32[]{:T(128)}, f32[512,128]{1,0:T(8,128)S(1)}, f32[4096,128]{1,0:T(8,128)S(1)}, f32[4096,128]{1,0:T(8,128)}, s32[]{:T(128)}, /*index=5*/s32[4096]...) while((s32[]{:T(128)}, f32[512,128]{1,0:T(8,128)S(1)}, ...), condition=%wide.region_20.20_spmd, body=%wide.region_17.19_spmd.sunk | while | flops 338887680 | bytes 7236137 | solution.py:119
  366.0 6.9 conditional.6
  374.8 6.9 conditional.6
  388.9 19.6 %while.130 = (s32[]{:T(128)}, f32[512,128]{1,0:T(8,128)S(1)}, f32[4096,128]{1,0:T(8,128)S(1)}, f32[4096,128]{1,0:T(8,128)}, s32[]{:T(128)}, /*index=5*/s32[4096]...) while((s32[]{:T(128)}, f32[512,128]{1,0:T(8,128)S(1)}, ...), condition=%wide.region_20.20_spmd, body=%wide.region_17.19_spmd.sunk | while | flops 338887680 | bytes 7236137 | solution.py:119
  392.8 6.9 conditional.6
  401.6 6.9 conditional.6
  415.7 28.4 %while.130 = (s32[]{:T(128)}, f32[512,128]{1,0:T(8,128)S(1)}, f32[4096,128]{1,0:T(8,128)S(1)}, f32[4096,128]{1,0:T(8,128)}, s32[]{:T(128)}, /*index=5*/s32[4096]...) while((s32[]{:T(128)}, f32[512,128]{1,0:T(8,128)S(1)}, ...), condition=%wide.region_20.20_spmd, body=%wide.region_17.19_spmd.sunk | while | flops 338887680 | bytes 7236137 | solution.py:119
  419.6 6.9 conditional.6
  428.4 6.9 conditional.6
  437.2 6.9 conditional.6
  451.3 23.5 %while.130 = (s32[]{:T(128)}, f32[512,128]{1,0:T(8,128)S(1)}, f32[4096,128]{1,0:T(8,128)S(1)}, f32[4096,128]{1,0:T(8,128)}, s32[]{:T(128)}, /*index=5*/s32[4096]...) while((s32[]{:T(128)}, f32[512,128]{1,0:T(8,128)S(1)}, ...), condition=%wide.region_20.20_spmd, body=%wide.region_17.19_spmd.sunk | while | flops 338887680 | bytes 7236137 | solution.py:119
  459.1 6.9 conditional.6
  467.9 6.9 conditional.6
  482.0 25.5 %while.130 = (s32[]{:T(128)}, f32[512,128]{1,0:T(8,128)S(1)}, f32[4096,128]{1,0:T(8,128)S(1)}, f32[4096,128]{1,0:T(8,128)}, s32[]{:T(128)}, /*index=5*/s32[4096]...) while((s32[]{:T(128)}, f32[512,128]{1,0:T(8,128)S(1)}, ...), condition=%wide.region_20.20_spmd, body=%wide.region_17.19_spmd.sunk | while | flops 338887680 | bytes 7236137 | solution.py:119
  491.8 6.9 conditional.6
  500.6 6.9 conditional.6
  514.7 27.4 %while.130 = (s32[]{:T(128)}, f32[512,128]{1,0:T(8,128)S(1)}, f32[4096,128]{1,0:T(8,128)S(1)}, f32[4096,128]{1,0:T(8,128)}, s32[]{:T(128)}, /*index=5*/s32[4096]...) while((s32[]{:T(128)}, f32[512,128]{1,0:T(8,128)S(1)}, ...), condition=%wide.region_20.20_spmd, body=%wide.region_17.19_spmd.sunk | while | flops 338887680 | bytes 7236137 | solution.py:119
  526.4 6.9 conditional.6
  549.3 29.4 %while.130 = (s32[]{:T(128)}, f32[512,128]{1,0:T(8,128)S(1)}, f32[4096,128]{1,0:T(8,128)S(1)}, f32[4096,128]{1,0:T(8,128)}, s32[]{:T(128)}, /*index=5*/s32[4096]...) while((s32[]{:T(128)}, f32[512,128]{1,0:T(8,128)S(1)}, ...), condition=%wide.region_20.20_spmd, body=%wide.region_17.19_spmd.sunk | while | flops 338887680 | bytes 7236137 | solution.py:119
  571.7 6.9 conditional.6
  582.2 9.8 %all-to-all-start.5 = ((bf16[32,128,128]{2,1,0:T(8,128)(2,1)}), bf16[32,128,128]{2,1,0:T(8,128)(2,1)}, u32[]{:S(2)}, u32[]{:S(2)}) async-start(bf16[32,128,128]{2,1,0:T(8,128)(2,1)} %bitcast.39), calls=%async_computation.5 | async-start | bytes 2097152 | tf_op jit(solution)/shard_map/all_to_all | solution.py:191
  593.9 18.6 %all-to-all-done.5 = bf16[32,128,128]{2,1,0:T(8,128)(2,1)} async-done(((bf16[32,128,128]{2,1,0:T(8,128)(2,1)}), bf16[32,128,128]{2,1,0:T(8,128)(2,1)}, u32[]{:S(2)}, u32[]{:S(2)}) %all-to-all-start.5) | async-done | bytes 1048608 | tf_op jit(solution)/shard_map/all_to_all | solution.py:191
  612.6 7.5 %all-to-all-start.6 = ((bf16[32,128,128]{2,1,0:T(8,128)(2,1)}), bf16[32,128,128]{2,1,0:T(8,128)(2,1)S(1)}, u32[]{:S(2)}, u32[]{:S(2)}) async-start(bf16[32,128,128]{2,1,0:T(8,128)(2,1)} %bitcast.142), calls=%async_computation.6 | async-start | bytes 2097152 | tf_op jit(solution)/shard_map/all_to_all | solution.py:194
  621.8 18.7 %all-to-all-done.6 = bf16[32,128,128]{2,1,0:T(8,128)(2,1)S(1)} async-done(((bf16[32,128,128]{2,1,0:T(8,128)(2,1)}), bf16[32,128,128]{2,1,0:T(8,128)(2,1)S(1)}, u32[]{:S(2)}, u32[]{:S(2)}) %all-to-all-start.6) | async-done | bytes 1048608 | tf_op jit(solution)/shard_map/all_to_all | solution.py:194
  640.4 9.5 %all-to-all-start.7 = ((bf16[32,128,128]{2,1,0:T(8,128)(2,1)}), bf16[32,128,128]{2,1,0:T(8,128)(2,1)S(1)}, u32[]{:S(2)}, u32[]{:S(2)}) async-start(bf16[32,128,128]{2,1,0:T(8,128)(2,1)} %bitcast.48), calls=%async_computation.7 | async-start | bytes 2097152 | tf_op jit(solution)/shard_map/all_to_all | solution.py:197
  652.8 19.7 %all-to-all-done.7 = bf16[32,128,128]{2,1,0:T(8,128)(2,1)S(1)} async-done(((bf16[32,128,128]{2,1,0:T(8,128)(2,1)}), bf16[32,128,128]{2,1,0:T(8,128)(2,1)S(1)}, u32[]{:S(2)}, u32[]{:S(2)}) %all-to-all-start.7) | async-done | bytes 1048608 | tf_op jit(solution)/shard_map/all_to_all | solution.py:197
  672.5 9.1 %all-to-all-start.3 = ((bf16[32,128,128]{2,1,0:T(8,128)(2,1)}), bf16[32,128,128]{2,1,0:T(8,128)(2,1)S(1)}, u32[]{:S(2)}, u32[]{:S(2)}) async-start(bf16[32,128,128]{2,1,0:T(8,128)(2,1)} %bitcast.30), calls=%async_computation.3 | async-start | bytes 2097152 | tf_op jit(solution)/shard_map/all_to_all | solution.py:190
  688.3 19.1 %all-to-all-done.3 = bf16[32,128,128]{2,1,0:T(8,128)(2,1)S(1)} async-done(((bf16[32,128,128]{2,1,0:T(8,128)(2,1)}), bf16[32,128,128]{2,1,0:T(8,128)(2,1)S(1)}, u32[]{:S(2)}, u32[]{:S(2)}) %all-to-all-start.3) | async-done | bytes 1048608 | tf_op jit(solution)/shard_map/all_to_all | solution.py:190
  (673 shorter events, 391.1 us)
Async XLA Ops:
  0.6 13.6 %copy-start = (bf16[128,512]{1,0:T(8,128)(2,1)S(1)}, bf16[128,512]{1,0:T(8,128)(2,1)}, u32[]{:S(2)}) copy-start(bf16[128,512]{1,0:T(8,128)(2,1)} %param.23) | copy-start | bytes 393220
  2.9 40.0 %all-to-all-start = ((bf16[128,32,128]{0,2,1:T(8,128)(2,1)}), bf16[128,32,128]{0,2,1:T(8,128)(2,1)S(1)}, u32[]{:S(2)}, u32[]{:S(2)}) async-start(bf16[128,32,128]{0,2,1:T(8,128)(2,1)} %bitcast.15), calls=%async_computation | async-start | bytes 2097152 | tf_op jit(solution)/shard_map/all_to_all | solution.py:146
  14.3 35.0 %copy-start.5 = (bf16[128,512]{1,0:T(8,128)(2,1)S(1)}, bf16[128,512]{1,0:T(8,128)(2,1)}, u32[]{:S(2)}) copy-start(bf16[128,512]{1,0:T(8,128)(2,1)} %param.24) | copy-start | bytes 393220
  42.9 35.9 %copy-start.4 = (bf16[128,32,128]{0,2,1:T(8,128)(2,1)}, bf16[128,32,128]{0,2,1:T(8,128)(2,1)S(1)}, u32[]{:S(2)}) copy-start(bf16[128,32,128]{0,2,1:T(8,128)(2,1)S(1)} %all-to-all-done) | copy-start | bytes 3145732
  44.2 33.4 %all-to-all-start.1 = ((bf16[128,32,128]{2,0,1:T(8,128)(2,1)}), bf16[128,32,128]{2,0,1:T(8,128)(2,1)S(1)}, u32[]{:S(2)}, u32[]{:S(2)}) async-start(bf16[128,32,128]{2,0,1:T(8,128)(2,1)} %bitcast.21), calls=%async_computation.1 | async-start | bytes 2097152 | tf_op jit(solution)/shard_map/all_to_all | solution.py:147
  49.3 34.6 %copy-start.7 = (s32[8]{0:T(128)S(1)}, s32[8]{0:T(128)}, u32[]{:S(2)}) copy-start(s32[8]{0:T(128)} %param.26) | copy-start | bytes 100
  78.8 7.6 %copy-start.8 = (s32[64]{0:T(128)S(1)}, s32[64]{0:T(128)}, u32[]{:S(2)}) copy-start(s32[64]{0:T(128)} %param.27) | copy-start | bytes 772
  78.8 33.3 %all-to-all-start.2 = ((bf16[128,32,128]{2,0,1:T(8,128)(2,1)}), bf16[128,32,128]{2,0,1:T(8,128)(2,1)S(1)}, u32[]{:S(2)}, u32[]{:S(2)}) async-start(bf16[128,32,128]{2,0,1:T(8,128)(2,1)} %bitcast.148), calls=%async_computation.2 | async-start | bytes 2097152 | tf_op jit(solution)/shard_map/all_to_all | solution.py:148
  112.2 222.7 %all-to-all-start.4 = ((bf16[128,32,128]{0,2,1:T(8,128)(2,1)}), bf16[128,32,128]{0,2,1:T(8,128)(2,1)}, u32[]{:S(2)}, u32[]{:S(2)}) async-start(bf16[128,32,128]{0,2,1:T(8,128)(2,1)} %bitcast.146), calls=%async_computation.4 | async-start | bytes 2097152 | tf_op jit(solution)/shard_map/all_to_all | solution.py:149
  334.9 3.9 copy-start.2
  334.9 3.9 copy-start.3
  341.6 237.8 %copy-start.6 = (s32[1024]{0:T(1024)S(1)}, s32[1024]{0:T(1024)}, u32[]{:S(2)}) copy-start(s32[1024]{0:T(1024)} %pad_clamp_fusion) | copy-start | bytes 12292
  582.2 30.4 %all-to-all-start.5 = ((bf16[32,128,128]{2,1,0:T(8,128)(2,1)}), bf16[32,128,128]{2,1,0:T(8,128)(2,1)}, u32[]{:S(2)}, u32[]{:S(2)}) async-start(bf16[32,128,128]{2,1,0:T(8,128)(2,1)} %bitcast.39), calls=%async_computation.5 | async-start | bytes 2097152 | tf_op jit(solution)/shard_map/all_to_all | solution.py:191
  592.2 27.9 %copy-start.1 = (f32[4096,128]{1,0:T(8,128)S(1)}, f32[4096,128]{1,0:T(8,128)}, u32[]{:S(2)}) copy-start(f32[4096,128]{1,0:T(8,128)} %get-tuple-element.1416) | copy-start | bytes 6291460
  612.6 27.9 %all-to-all-start.6 = ((bf16[32,128,128]{2,1,0:T(8,128)(2,1)}), bf16[32,128,128]{2,1,0:T(8,128)(2,1)S(1)}, u32[]{:S(2)}, u32[]{:S(2)}) async-start(bf16[32,128,128]{2,1,0:T(8,128)(2,1)} %bitcast.142), calls=%async_computation.6 | async-start | bytes 2097152 | tf_op jit(solution)/shard_map/all_to_all | solution.py:194
  640.4 32.1 %all-to-all-start.7 = ((bf16[32,128,128]{2,1,0:T(8,128)(2,1)}), bf16[32,128,128]{2,1,0:T(8,128)(2,1)S(1)}, u32[]{:S(2)}, u32[]{:S(2)}) async-start(bf16[32,128,128]{2,1,0:T(8,128)(2,1)} %bitcast.48), calls=%async_computation.7 | async-start | bytes 2097152 | tf_op jit(solution)/shard_map/all_to_all | solution.py:197
  672.5 34.9 %all-to-all-start.3 = ((bf16[32,128,128]{2,1,0:T(8,128)(2,1)}), bf16[32,128,128]{2,1,0:T(8,128)(2,1)S(1)}, u32[]{:S(2)}, u32[]{:S(2)}) async-start(bf16[32,128,128]{2,1,0:T(8,128)(2,1)} %bitcast.30), calls=%async_computation.3 | async-start | bytes 2097152 | tf_op jit(solution)/shard_map/all_to_all | solution.py:190
where the time goes:
time: 720 us; the launch traced here: 709 us
  loops' own time  200 us (28%)
  waiting for transfers between devices  152 us (21%)
  local copies, waits for them, and re-layouts  147 us (20%)
  matrix products  118 us (16%)
  starting transfers between devices  62.5 us (9%)
  other arithmetic  28.8 us (4%)
    dynamic_slice x124, local copies, waits for them, and re-layouts, is_live(): return docs[col_blk * BLK + BLK - 1] >= docs[row_blk * BLK]  79.9 us
    another operation x8, loops' own time, backward_one_block(): q_grad, k_grad, v_grad = lax.fori_loop(0, row_blk + 1, step, start)  46.2 us
    another operation x8, loops' own time, forward_one_block(): top, total = lax.fori_loop(0, row_blk + 1, stats, start)  44.2 us
    another operation x8, loops' own time, forward_one_block(): lax.fori_loop(0, row_blk + 1, add_values, jnp.zeros((BLK, q_place.shape[1...  44.2 us
    dot_general x16, matrix products, step_live(): jnp.einsum('qk,qd->kd', rounded, g_block, preferred_element_type=jnp.floa...  31.4 us
    all_to_all x1, waiting for transfers between devices, on_device(): lax.all_to_all(queries, 'seq', split_axis=1, concat_axis=0, tiled=True)  28.6 us
    dot_general x32, matrix products, block_scores(): jnp.dot(q_block, k_block.T, preferred_element_type=jnp.float32) * scale  28.4 us
    all_to_all x1, waiting for transfers between devices, on_device(): lax.all_to_all(k_wide, 'seq', split_axis=1, concat_axis=0, tiled=True)  28.2 us
  transfers between devices with their start and end apart: 8, of which 7 were waited for; matrix products, arithmetic and copies ran while one was open for 17% of the time, Pallas kernels for 0%

commit v1 on v0

v1 whole, which is shorter than its diff:
```python
import functools
import math

import jax
import jax.numpy as jnp
from jax import lax
from jax.experimental import pallas as pl
from jax.experimental.pallas import tpu as pltpu
from jax.sharding import PartitionSpec as P

NX = 4
NZ = 8
ROWS = 128
SPAN = 64
HEAD = 128
GROUP = 8
WIDE = GROUP * HEAD
SPANS = 64
REACH = 16
MESH = pl.DeviceIdType.MESH
SCALE = HEAD ** -0.5
NEG = -1e30
BF = jnp.bfloat16
F32 = jnp.float32


def place():
    me = lax.axis_index("seq")
    return me // NZ, lax.rem(me, NZ)


def device(x, z):
    return {"seq": lax.rem(x + NX, NX) * NZ + lax.rem(z + NZ, NZ)}


def enter(x, z):
    barrier = pltpu.get_barrier_semaphore()
    partners = [device(x + d, z) for d in (1, 2, 3)] + [device(x, z + 1), device(x, z - 1)]
    for partner in partners:
        pl.semaphore_signal(barrier, inc=1, device_id=partner, device_id_type=MESH)
    pl.semaphore_wait(barrier, len(partners))


def columns(index, width):
    return pl.ds(pl.multiple_of(index * width, width), width)


def ring(arrays):
    return [(a, d, NZ // 2 if a == d else NZ // 2 - 1) for a in range(arrays) for d in (0, 1)]


def gather_kernel(q_ref, k_ref, v_ref, g_ref, qo_ref, ko_ref, vo_ref, go_ref,
                  own_sem, send_sem, recv_sem, ring_send, ring_recv):
    x, z = place()
    enter(x, z)
    sources = [k_ref, v_ref, q_ref, g_ref]
    widths = [HEAD, HEAD, WIDE, WIDE]
    targets = [ko_ref.at[z, x], vo_ref.at[z, x], qo_ref.at[x], go_ref.at[x]]
    copies, local = [], []
    for a in range(4):
        own = pltpu.make_async_copy(sources[a].at[:, columns(x, widths[a])], targets[a], own_sem.at[a])
        own.start()
        local.append(own)
        row = []
        for d in (1, 3, 2):
            to = lax.rem(x + d, NX)
            copy = pltpu.make_async_remote_copy(
                src_ref=sources[a].at[:, columns(to, widths[a])],
                dst_ref=targets[a],
                send_sem=send_sem.at[a, d - 1],
                recv_sem=recv_sem.at[a, d - 1],
                device_id=device(to, z),
                device_id_type=MESH,
            )
            copy.start()
            row.append(copy)
        copies.append(row)

    outs = [ko_ref, vo_ref]

    def hop(a, d, step):
        sign = 1 - 2 * d
        block = lax.rem(z - sign * step + NZ, NZ)
        return pltpu.make_async_remote_copy(
            src_ref=outs[a].at[block],
            dst_ref=outs[a].at[block],
            send_sem=ring_send.at[a, d, step],
            recv_sem=ring_recv.at[a, d, step],
            device_id=device(x, z + sign),
            device_id_type=MESH,
        )

    hops = {}
    for a in range(2):
        local[a].wait()
        for copy in copies[a]:
            copy.wait_recv()
        for d in range(2):
            hops[a, d, 0] = hop(a, d, 0)
            hops[a, d, 0].start()
    for step in range(1, NZ // 2 + 1):
        for a, d, count in ring(2):
            if step <= count:
                hops[a, d, step - 1].wait_recv()
            if step < count:
                hops[a, d, step] = hop(a, d, step)
                hops[a, d, step].start()
    for a in (2, 3):
        local[a].wait()
        for copy in copies[a]:
            copy.wait_recv()
    for row in copies:
        for copy in row:
            copy.wait_send()
    for copy in hops.values():
        copy.wait_send()


def scatter_kernel(o_ref, dq_ref, dk_ref, dv_ref, oo_ref, dqo_ref, dko_ref, dvo_ref,
                   outgoing, incoming, total, own_sem, send_sem, recv_sem, ring_send, ring_recv):
    x, z = place()
    enter(x, z)
    sources = [total.at[0], total.at[1], o_ref, dq_ref]
    widths = [HEAD, HEAD, WIDE, WIDE]
    targets = [dko_ref, dvo_ref, oo_ref, dqo_ref]
    copies, local = [], []

    def exchange(a):
        mine = targets[a].at[:, columns(x, widths[a])]
        own = pltpu.make_async_copy(sources[a].at[x], mine, own_sem.at[a])
        own.start()
        local.append(own)
        for d in (1, 3, 2):
            to = lax.rem(x + d, NX)
            copy = pltpu.make_async_remote_copy(
                src_ref=sources[a].at[to],
                dst_ref=mine,
                send_sem=send_sem.at[a, d - 1],
                recv_sem=recv_sem.at[a, d - 1],
                device_id=device(to, z),
                device_id_type=MESH,
            )
            copy.start()
            copies.append(copy)

    terms = [dk_ref, dv_ref]

    def hop(a, d, step):
        sign = 1 - 2 * d
        return pltpu.make_async_remote_copy(
            src_ref=outgoing.at[a, d, step],
            dst_ref=incoming.at[a, d, step],
            send_sem=ring_send.at[a, d, step],
            recv_sem=ring_recv.at[a, d, step],
            device_id=device(x, z + sign),
            device_id_type=MESH,
        )

    hops = {}
    for step in range(NZ // 2 + 1):
        for a, d, count in ring(2):
            if step > count:
                continue
            if step > 0:
                hops[a, d, step - 1].wait_recv()
            if step < count:
                sign = 1 - 2 * d
                block = lax.rem(z + sign * (count - step) + NZ, NZ)
                value = terms[a][block]
                if step > 0:
                    value = value + incoming[a, d, step - 1].astype(F32)
                outgoing[a, d, step] = value.astype(BF)
                hops[a, d, step] = hop(a, d, step)
                hops[a, d, step].start()
        if step == 0:
            exchange(2)
            exchange(3)
    for a in range(2):
        value = terms[a][z]
        for b, d, count in ring(2):
            if a == b:
                value = value + incoming[a, d, count - 1].astype(F32)
        total[a] = value.astype(BF)
        exchange(a)
    for copy in local:
        copy.wait()
    for copy in copies:
        copy.wait()
    for copy in hops.values():
        copy.wait_send()


def attend_kernel(order_ref, length_ref, q_ref, g_ref, k_ref, v_ref, o_ref, dq_ref, dk_ref, dv_ref,
                  kpos, vpos, dka, dva):
    _, z = place()
    pad = REACH * SPAN
    kpos[:pad] = jnp.zeros((pad, HEAD), BF)
    vpos[:pad] = jnp.zeros((pad, HEAD), BF)
    dka[...] = jnp.zeros(dka.shape, F32)
    dva[...] = jnp.zeros(dva.shape, F32)

    def slot(u):
        zz, rest = u // (2 * NX), lax.rem(u, 2 * NX)
        return 2 * (rest // 2 * NZ + zz) + lax.rem(rest, 2)

    def rows(position):
        return pl.ds(pl.multiple_of((position + REACH) * SPAN, SPAN), SPAN)

    @pl.loop(0, SPANS)
    def _(u):
        here = rows(order_ref[slot(u)])
        kpos[here] = k_ref[u]
        vpos[here] = v_ref[u]

    starts = []
    total = length_ref[0]
    for i in range(1, 8):
        starts.append(total)
        total = total + length_ref[i]

    @pl.loop(0, 2 * NX)
    def _(s):
        xx, half = s // 2, lax.rem(s, 2)
        c = order_ref[2 * (xx * NZ + z) + half]
        lane = lax.broadcasted_iota(jnp.int32, (1, HEAD), 1)
        rp = c * SPAN + lax.rem(lane, SPAN)
        rs = jnp.zeros((1, HEAD), jnp.int32)
        first = jnp.int32(0)
        for start in starts:
            rs = jnp.where(rp >= start, start, rs)
            first = jnp.where(c * SPAN >= start, start, first)
        need = c - first // SPAN + 1
        mine = pl.ds(pl.multiple_of(half * SPAN, SPAN), SPAN)

        def work(width):
            base = pl.multiple_of((c + REACH + 1) * SPAN - width, SPAN)
            window = pl.ds(base, width)
            kp = base - pad + lax.broadcasted_iota(jnp.int32, (width, HEAD), 0)
            seen = (kp >= rs) & (kp <= rp)
            heads = 4
            wide_seen = jnp.concatenate([seen] * (heads // 2), axis=1)

            @pl.loop(0, GROUP // heads)
            def _(part):
                def stacked(ref):
                    return jnp.concatenate(
                        [ref[xx, mine, pl.ds(pl.multiple_of((part * heads + h) * HEAD, HEAD), HEAD)]
                         for h in range(heads)], axis=0)

                kw, vw = kpos[window], vpos[window]
                q, g = stacked(q_ref), stacked(g_ref)
                s_t = lax.dot_general(kw, q, (((1,), (1,)), ((), ())), preferred_element_type=F32)
                s_t = jnp.where(wide_seen, s_t * (SCALE * math.log2(math.e)), NEG)
                e = jnp.exp2(s_t - jnp.max(s_t, axis=0, keepdims=True))
                p = e * (1.0 / jnp.sum(e, axis=0, keepdims=True))
                pb = p.astype(BF)
                o_t = lax.dot_general(vw, pb, (((0,), (0,)), ((), ())), preferred_element_type=F32)
                dva[window] += jnp.dot(pb, g, preferred_element_type=F32)
                dp = lax.dot_general(vw, g, (((1,), (1,)), ((), ())), preferred_element_type=F32)
                delta = jnp.sum(p * dp, axis=0, keepdims=True)
                ds = (p * (dp - delta)).astype(BF)
                dq_t = lax.dot_general(kw, ds, (((0,), (0,)), ((), ())), preferred_element_type=F32)
                dka[window] += jnp.dot(ds, q, preferred_element_type=F32)
                o = o_t.T.astype(BF)
                dq = (dq_t.T * SCALE).astype(BF)
                for h in range(heads):
                    cols = pl.ds(pl.multiple_of((part * heads + h) * HEAD, HEAD), HEAD)
                    o_ref[xx, mine, cols] = o[h * SPAN:(h + 1) * SPAN]
                    dq_ref[xx, mine, cols] = dq[h * SPAN:(h + 1) * SPAN]

        below = 0
        for width in (256, 512, 768, (REACH + 1) * SPAN):
            pl.when((need * SPAN > below) & (need * SPAN <= width))(functools.partial(work, width))
            below = width

    @pl.loop(0, SPANS)
    def _(u):
        here = rows(order_ref[slot(u)])
        dk_ref[u] = dka[here] * SCALE
        dv_ref[u] = dva[here]


def on_device(queries, keys, values, out_grad, doc_lengths, span_order):
    any_spec = pl.BlockSpec(memory_space=pl.ANY)
    vmem = pl.BlockSpec(memory_space=pltpu.VMEM)
    smem = pl.BlockSpec(memory_space=pltpu.SMEM)
    dma = pltpu.SemaphoreType.DMA
    heads_shape = jax.ShapeDtypeStruct((NX, ROWS, WIDE), BF)
    kv_shape = jax.ShapeDtypeStruct((NZ, NX, ROWS, HEAD), BF)
    sems = [dma((4,)), dma((4, 3)), dma((4, 3)), dma((2, 2, 4)), dma((2, 2, 4))]
    q, k, v, g = pl.pallas_call(
        gather_kernel,
        out_shape=[heads_shape, kv_shape, kv_shape, heads_shape],
        in_specs=[any_spec] * 4,
        out_specs=[any_spec] * 4,
        scratch_shapes=sems,
        compiler_params=pltpu.CompilerParams(collective_id=0, has_side_effects=True),
        name="gather",
    )(queries, keys, values, out_grad)

    spans_shape = (SPANS, SPAN, HEAD)
    sum_shape = jax.ShapeDtypeStruct(spans_shape, F32)
    padded = ((SPANS + REACH) * SPAN, HEAD)
    o, dq, dk, dv = pl.pallas_call(
        attend_kernel,
        out_shape=[heads_shape, heads_shape, sum_shape, sum_shape],
        in_specs=[smem, smem] + [vmem] * 4,
        out_specs=[vmem] * 4,
        scratch_shapes=[pltpu.VMEM(padded, BF)] * 2 + [pltpu.VMEM(padded, F32)] * 2,
        compiler_params=pltpu.CompilerParams(vmem_limit_bytes=56 * 2 ** 20),
        name="attend",
    )(span_order, doc_lengths, q, g, k.reshape(spans_shape), v.reshape(spans_shape))

    terms_shape = (NZ, NX, ROWS, HEAD)
    return pl.pallas_call(
        scatter_kernel,
        out_shape=[
            jax.ShapeDtypeStruct((ROWS, NX * WIDE), BF),
            jax.ShapeDtypeStruct((ROWS, NX * WIDE), BF),
            jax.ShapeDtypeStruct((ROWS, NX * HEAD), BF),
            jax.ShapeDtypeStruct((ROWS, NX * HEAD), BF),
        ],
        in_specs=[any_spec, any_spec, vmem, vmem],
        out_specs=[any_spec] * 4,
        scratch_shapes=[
            pltpu.VMEM((2, 2, 4, NX, ROWS, HEAD), BF),
            pltpu.VMEM((2, 2, 4, NX, ROWS, HEAD), BF),
            pltpu.VMEM((2, NX, ROWS, HEAD), BF),
        ] + sems,
        compiler_params=pltpu.CompilerParams(
            collective_id=1, has_side_effects=True, vmem_limit_bytes=32 * 2 ** 20),
        name="scatter",
    )(o, dq, dk.reshape(terms_shape), dv.reshape(terms_shape))


def solution(mesh):
    rows = P(("grp", "seq"), None)
    return jax.shard_map(
        on_device,
        mesh=mesh,
        in_specs=(rows, rows, rows, rows, P("grp"), P("grp")),
        out_specs=(rows, rows, rows, rows),
        check_vma=False,
    )
```

time: 720 us -> 103 us (0.14); the launches traced: 709 us -> 103 us
  loops' own time: 200 us -> 0 us
  waiting for transfers between devices: 152 us -> 0 us
  local copies, waits for them, and re-layouts: 147 us -> 8.88 us
  matrix products: 118 us -> 0 us
  Pallas kernels: 0 us -> 93.3 us
  starting transfers between devices: 62.5 us -> 0 us
  other arithmetic: 28.8 us -> 0 us
    another operation x134 -> x0, loops' own time: 200 us -> none  [the longest x8 46.2 us: backward_one_block(): q_grad, k_grad, v_grad = lax.fori_loop(0, row_blk + 1, step, start)]
    all_to_all x8 -> x0, waiting for transfers between devices: 152 us -> none  [the longest x1 28.6 us: on_device(): lax.all_to_all(queries, 'seq', split_axis=1, concat_axis=0, tiled=True)]
    dot_general x112 -> x0, matrix products: 118 us -> none  [the longest x16 31.4 us: step_live(): jnp.einsum('qk,qd->kd', rounded, g_block, preferred_element_type=jnp.floa...]
    dynamic_slice x212 -> x0, local copies, waits for them, and re-layouts: 109 us -> none  [the longest x124 79.9 us: is_live(): return docs[col_blk * BLK + BLK - 1] >= docs[row_blk * BLK]]
    pallas_call x0 -> x3, Pallas kernels: none -> 93.3 us  [the longest x1 35.7 us: on_device(): pl.pallas_call(gather_kernel, out_shape=[heads_shape, kv_shape, kv_shape,...]
    all_to_all x8 -> x0, starting transfers between devices: 62.5 us -> none  [the longest x1 11.3 us: on_device(): lax.all_to_all(queries, 'seq', split_axis=1, concat_axis=0, tiled=True)]
    reduce_sum x27 -> x0, other arithmetic: 14.4 us -> none  [the longest x8 8.96 us: backward_one_block(): jnp.sum(o_block.astype(jnp.float32) * g_block.astype(jnp.float32), axis=1)]
    gather x8 -> x0, local copies, waits for them, and re-layouts: 13.9 us -> none  [the longest x4 9.08 us: into_layout(): block_tile.reshape(spans, half, block_tile.shape[1])[span_order]]
  transfers between devices with their start and end apart: 8 -> 0, of which waited for: 7 -> 0; matrix products, arithmetic and copies ran while one was open for 17% -> 0% of each run, Pallas kernels for 0% -> 0%
where the time goes in v1:
time: 103 us
  Pallas kernels  93.3 us (91%)
  local copies, waits for them, and re-layouts  8.88 us (9%)
    pallas_call x1, Pallas kernels, on_device(): pl.pallas_call(gather_kernel, out_shape=[heads_shape, kv_shape, kv_shape,...  35.7 us
    pallas_call x1, Pallas kernels, on_device(): pl.pallas_call(scatter_kernel, out_shape=[jax.ShapeDtypeStruct((ROWS, NX...  33 us
    pallas_call x1, Pallas kernels, on_device(): pl.pallas_call(attend_kernel, out_shape=[heads_shape, heads_shape, sum_sh...  24.6 us
    unnamed x12, local copies, waits for them, and re-layouts  8.88 us

profile of v1, /device:TPU:8, one launch (start us, length us, event | category | flops | bytes accessed | tf_op | source)
XLA Modules:
  0.0 102.9 jit_solution(12435456532441220183)
XLA Ops:
  0.6 35.7 %gather.1 = (bf16[4,128,1024]{2,1,0:T(8,128)(2,1)}, bf16[8,4,128,128]{3,2,1,0:T(8,128)(2,1)}, bf16[8,4,128,128]{3,2,1,0:T(8,128)(2,1)}, bf16[4,128,1024]{2,1,0:T(8,128)(2,1)}) custom-call(bf16[128,4096]{1,0:T(8,128)(2,1)} %q_ref.1, bf16[128,512]{1,0:T(8,128)(2,1)} %k_ref.1, bf16[128,512]{1,0:T(8,128)(2,1)} %v_ref.1, bf16[128,4096]{1,0:T(8,128)(2,1)} %g_ref.1), custom_call_target="tpu_custom_call" | custom-call | tf_op jit(solution)/shard_map/gather/pallas_call | solution.py:291
  36.4 24.6 %attend.1 = (bf16[4,128,1024]{2,1,0:T(8,128)(2,1)}, bf16[4,128,1024]{2,1,0:T(8,128)(2,1)}, f32[64,64,128]{2,1,0:T(8,128)}, f32[64,64,128]{2,1,0:T(8,128)}) custom-call(s32[64]{0:T(128)} %order_ref.1, s32[8]{0:T(128)} %length_ref.1, bf16[4,128,1024]{2,1,0:T(8,128)(2,1)} %get-tuple-element.12.q_ref, bf16[4,128,1024]{2,1,0:T(8,128)(2,1)} %get-tuple-element.13.g_ref, ...), custom_call_target="tpu_custom_call" | custom-call | tf_op jit(solution)/shard_map/attend/pallas_call | solution.py:304
  61.0 0.0 copy-start
  61.0 1.6 %copy-done = f32[64,64,128]{2,1,0:T(8,128)S(1)} copy-done((f32[64,64,128]{2,1,0:T(8,128)S(1)}, f32[64,64,128]{2,1,0:T(8,128)}, u32[]{:S(2)}) %copy-start) | copy-done | bytes 2097176
  62.6 0.0 copy-start.1
  62.6 1.6 %copy-done.1 = f32[64,64,128]{2,1,0:T(8,128)S(1)} copy-done((f32[64,64,128]{2,1,0:T(8,128)S(1)}, f32[64,64,128]{2,1,0:T(8,128)}, u32[]{:S(2)}) %copy-start.1) | copy-done | bytes 2097176
  64.1 0.0 copy-start.2
  64.2 1.2 %copy-done.2 = bf16[4,128,1024]{2,1,0:T(8,128)(2,1)S(1)} copy-done((bf16[4,128,1024]{2,1,0:T(8,128)(2,1)S(1)}, bf16[4,128,1024]{2,1,0:T(8,128)(2,1)}, u32[]{:S(2)}) %copy-start.2) | copy-done | bytes 1048600
  65.4 0.0 copy-start.3
  65.4 1.2 %copy-done.3 = bf16[4,128,1024]{2,1,0:T(8,128)(2,1)S(1)} copy-done((bf16[4,128,1024]{2,1,0:T(8,128)(2,1)S(1)}, bf16[4,128,1024]{2,1,0:T(8,128)(2,1)}, u32[]{:S(2)}) %copy-start.3) | copy-done | bytes 1048600
  66.6 33.0 %scatter.1 = (bf16[128,4096]{1,0:T(8,128)(2,1)S(1)}, bf16[128,4096]{1,0:T(8,128)(2,1)S(1)}, bf16[128,512]{1,0:T(8,128)(2,1)S(1)}, bf16[128,512]{1,0:T(8,128)(2,1)S(1)}) custom-call(bf16[4,128,1024]{2,1,0:T(8,128)(2,1)S(1)} %copy-done.2, bf16[4,128,1024]{2,1,0:T(8,128)(2,1)S(1)} %copy-done.3, f32[8,4,128,128]{3,2,1,0:T(8,128)S(1)} %bitcast.4, ...), custom_call_target="tpu_custom_call" | custom-call | tf_op jit(solution)/shard_map/scatter/pallas_call | solution.py:315
  99.6 1.0 copy.14
  100.6 1.0 copy.15
  101.6 0.7 copy.16
  102.2 0.7 copy.17
Async XLA Ops:
  61.0 1.6 %copy-start = (f32[64,64,128]{2,1,0:T(8,128)S(1)}, f32[64,64,128]{2,1,0:T(8,128)}, u32[]{:S(2)}) copy-start(f32[64,64,128]{2,1,0:T(8,128)} %get-tuple-element.18) | copy-start | bytes 6291460
  62.6 1.6 %copy-start.1 = (f32[64,64,128]{2,1,0:T(8,128)S(1)}, f32[64,64,128]{2,1,0:T(8,128)}, u32[]{:S(2)}) copy-start(f32[64,64,128]{2,1,0:T(8,128)} %get-tuple-element.19) | copy-start | bytes 6291460
  64.1 1.2 %copy-start.2 = (bf16[4,128,1024]{2,1,0:T(8,128)(2,1)S(1)}, bf16[4,128,1024]{2,1,0:T(8,128)(2,1)}, u32[]{:S(2)}) copy-start(bf16[4,128,1024]{2,1,0:T(8,128)(2,1)} %get-tuple-element.16.o_ref) | copy-start | bytes 3145732
  65.4 1.2 %copy-start.3 = (bf16[4,128,1024]{2,1,0:T(8,128)(2,1)S(1)}, bf16[4,128,1024]{2,1,0:T(8,128)(2,1)}, u32[]{:S(2)}) copy-start(bf16[4,128,1024]{2,1,0:T(8,128)(2,1)} %get-tuple-element.17.dq_ref) | copy-start | bytes 3145732

commit v2 on v0

v2 whole, which is shorter than its diff:
```python
import math

import jax
import jax.numpy as jnp
from jax import lax
from jax.experimental import pallas as pl
from jax.experimental.pallas import tpu as pltpu
from jax.sharding import PartitionSpec as P

NX = 4
NZ = 8
ROWS = 128
SPAN = 64
HEAD = 128
GROUP = 8
WIDE = GROUP * HEAD
SPANS = 64
REACH = 16
PAD = REACH * SPAN
WINDOW = PAD + SPAN
UNITS = 2 * NX
MESH = pl.DeviceIdType.MESH
SCALE = HEAD ** -0.5
NEG = -1e30
BF = jnp.bfloat16
F32 = jnp.float32


def columns(index, width):
    return pl.ds(pl.multiple_of(index * width, width), width)


def product(a, b, contract):
    return lax.dot_general(a, b, ((contract[0], contract[1]), ((), ())), preferred_element_type=F32)


def hop_count(d, j):
    return NZ // 2 if j == d else NZ // 2 - 1


LANES = [(d, j) for j in range(2) for d in range(2)]


def kernel(order_ref, slot_ref, length_ref, q_ref, k_ref, v_ref, g_ref, oo_ref, dqo_ref, dko_ref, dvo_ref,
           qx, gx, kx, vx, kpos, vpos, probs, dkw, dvw, ost, dqst,
           outgoing, incoming, total,
           own_in, send_in, recv_in, own_out, send_out, recv_out, own_fin, send_fin, recv_fin,
           gather_send, gather_recv, ring_send, ring_recv):
    me = lax.axis_index("seq")
    x, z = me // NZ, lax.rem(me, NZ)

    def device(xx, zz):
        return {"seq": lax.rem(xx + NX, NX) * NZ + lax.rem(zz + NZ, NZ)}

    barrier = pltpu.get_barrier_semaphore()
    partners = [device(x + d, z) for d in (1, 2, 3)] + [device(x, z + 1), device(x, z - 1)]
    for partner in partners:
        pl.semaphore_signal(barrier, inc=1, device_id=partner, device_id_type=MESH)
    pl.semaphore_wait(barrier, len(partners))

    sources = [k_ref, v_ref, q_ref, g_ref]
    here = pl.ds((z * NX + x) * 2, 2)
    landing = [kx.at[here], vx.at[here], qx.at[x], gx.at[x]]
    widths = [HEAD, HEAD, WIDE, WIDE]
    inward = []

    def outgoing_columns(a, to):
        return sources[a].at[:, :, columns(to, widths[a])] if a < 2 else sources[a].at[:, columns(to, widths[a])]

    for a in range(4):
        row = [pltpu.make_async_copy(outgoing_columns(a, x), landing[a], own_in.at[a])]
        for d in (1, 3, 2):
            to = lax.rem(x + d, NX)
            row.append(pltpu.make_async_remote_copy(
                src_ref=outgoing_columns(a, to),
                dst_ref=landing[a],
                send_sem=send_in.at[a, d - 1],
                recv_sem=recv_in.at[a, d - 1],
                device_id=device(to, z),
                device_id_type=MESH,
            ))
        for copy in row:
            copy.start()
        inward.append(row)

    def arrived(a):
        inward[a][0].wait()
        for copy in inward[a][1:]:
            copy.wait_recv()

    gathered = [kx, vx]
    gather_hops = {}

    def gather_step(a, step):
        for d, j in LANES:
            count = hop_count(d, j)
            if 0 < step <= count:
                gather_hops[a, d, j, step - 1].wait_recv()
            if step < count:
                sign = 1 - 2 * d
                begin = lax.rem(z - sign * step + NZ, NZ) * 2 * NX + 4 * j
                block = gathered[a].at[pl.ds(begin, 4)]
                gather_hops[a, d, j, step] = pltpu.make_async_remote_copy(
                    src_ref=block,
                    dst_ref=block,
                    send_sem=gather_send.at[a, d, j, step],
                    recv_sem=gather_recv.at[a, d, j, step],
                    device_id=device(x, z + sign),
                    device_id_type=MESH,
                )
                gather_hops[a, d, j, step].start()

    arrived(0)
    gather_step(0, 0)

    kpos[:REACH] = jnp.zeros((REACH, SPAN, HEAD), BF)
    vpos[:REACH] = jnp.zeros((REACH, SPAN, HEAD), BF)
    for unit in range(UNITS):
        dkw[unit, 0] = jnp.zeros((SPAN, HEAD), F32)
        dkw[unit, REACH + 2] = jnp.zeros((SPAN, HEAD), F32)
        dvw[unit, 0] = jnp.zeros((SPAN, HEAD), F32)
        dvw[unit, REACH + 2] = jnp.zeros((SPAN, HEAD), F32)

    gather_step(0, 1)
    arrived(1)
    gather_step(0, 2)
    gather_step(0, 3)
    gather_step(1, 0)
    gather_step(0, 4)

    def into_positions(source, target):
        @pl.loop(0, SPANS)
        def _(p):
            target[p + REACH] = source[slot_ref[p]]

    def unit_place(i):
        xx = lax.rem(x + 1 + i // 2, NX)
        return xx, lax.rem(i, 2)

    def unit_span(i):
        xx, half = unit_place(i)
        return order_ref[2 * (xx * NZ + z) + half]

    def window(ref, i):
        c = unit_span(i)
        return jnp.concatenate([ref[c + j] for j in range(REACH + 1)], axis=0)

    def stacked(ref, i):
        xx, half = unit_place(i)
        rows = pl.ds(pl.multiple_of(half * SPAN, SPAN), SPAN)
        return jnp.concatenate([ref[xx, rows, h * HEAD:(h + 1) * HEAD] for h in range(GROUP)], axis=0)

    starts = []
    running = length_ref[0]
    for i in range(1, 8):
        starts.append(running)
        running = running + length_ref[i]

    def weigh(i):
        c = unit_span(i)
        row = c * SPAN + lax.rem(lax.broadcasted_iota(jnp.int32, (1, HEAD), 1), SPAN)
        first = jnp.zeros((1, HEAD), jnp.int32)
        for start in starts:
            first = jnp.where(row >= start, start, first)
        key = (c - REACH) * SPAN + lax.broadcasted_iota(jnp.int32, (WINDOW, HEAD), 0)
        seen = (key >= first) & (key <= row)
        scores = product(window(kpos, i), stacked(qx, i), ((1,), (1,)))
        scores = jnp.where(jnp.concatenate([seen] * (GROUP // 2), axis=1), scores * (SCALE * math.log2(math.e)), NEG)
        weights = jnp.exp2(scores - jnp.max(scores, axis=0, keepdims=True))
        probs[i] = (weights * (1.0 / jnp.sum(weights, axis=0, keepdims=True))).astype(BF)

    def value_terms(i):
        dvw[i, 1:REACH + 2] = jnp.dot(
            probs[i], stacked(gx, i), preferred_element_type=F32).reshape(REACH + 1, SPAN, HEAD)

    def put_heads(target, i, value_t):
        value = value_t.T.astype(BF)
        for h in range(GROUP):
            target[i, :, h * HEAD:(h + 1) * HEAD] = value[h * SPAN:(h + 1) * SPAN]

    staged = [ost, dqst]
    results = [oo_ref, dqo_ref]

    def outward(a, i):
        xx, half = unit_place(i)
        rows = pl.ds(pl.multiple_of(half * SPAN, SPAN), SPAN)
        return pltpu.make_async_remote_copy(
            src_ref=staged[a].at[i],
            dst_ref=results[a].at[rows, columns(x, WIDE)],
            send_sem=send_out.at[a, i],
            recv_sem=recv_out.at[a, i],
            device_id=device(xx, z),
            device_id_type=MESH,
        )

    def keep(a, half):
        rows = pl.ds(half * SPAN, SPAN)
        return pltpu.make_async_copy(
            staged[a].at[UNITS - 2 + half], results[a].at[rows, columns(x, WIDE)], own_out.at[a, half])

    def leave(a, i):
        @pl.when(i < UNITS - 2)
        def _():
            outward(a, i).start()

    def attend(i):
        put_heads(ost, i, product(window(vpos, i), probs[i], ((0,), (0,))))
        leave(0, i)

    def slope(i):
        pressure = product(window(vpos, i), stacked(gx, i), ((1,), (1,)))
        p = probs[i].astype(F32)
        delta = jnp.sum(p * pressure, axis=0, keepdims=True)
        slopes = (p * (pressure - delta)).astype(BF)
        probs[i] = slopes
        dkw[i, 1:REACH + 2] = jnp.dot(
            slopes, stacked(qx, i), preferred_element_type=F32).reshape(REACH + 1, SPAN, HEAD)

    def query_grad(i):
        put_heads(dqst, i, product(window(kpos, i), probs[i], ((0,), (0,))) * SCALE)
        leave(1, i)

    terms = [dkw, dvw]
    factors = [SCALE, 1.0]
    ring_hops = {}

    def add_up(a, block, j, arriving, target):
        spans = [unit_span(i) for i in range(UNITS)]

        @pl.loop(0, 4)
        def _(u):
            xi, half = u // 2, lax.rem(u, 2)
            position = order_ref[2 * ((2 * j + xi) * NZ + block) + half]
            value = jnp.zeros((SPAN, HEAD), F32)
            for i in range(UNITS):
                away = jnp.clip(position - spans[i] + REACH + 1, 0, REACH + 2)
                value += terms[a][i, away]
            value *= factors[a]
            rows = pl.ds(pl.multiple_of(half * SPAN, SPAN), SPAN)
            for ref in arriving:
                value += ref[xi, rows].astype(F32)
            target[xi, rows] = value.astype(BF)

    def ring_step(a, step):
        for d, j in LANES:
            count = hop_count(d, j)
            if 0 < step <= count:
                ring_hops[a, d, j, step - 1].wait_recv()
            if step < count:
                sign = 1 - 2 * d
                arriving = [incoming.at[a, d, j, step - 1]] if step > 0 else []
                add_up(a, lax.rem(z + sign * (count - step) + NZ, NZ), j, arriving, outgoing.at[a, d, j, step])
                ring_hops[a, d, j, step] = pltpu.make_async_remote_copy(
                    src_ref=outgoing.at[a, d, j, step],
                    dst_ref=incoming.at[a, d, j, step],
                    send_sem=ring_send.at[a, d, j, step],
                    recv_sem=ring_recv.at[a, d, j, step],
                    device_id=device(x, z + sign),
                    device_id_type=MESH,
                )
                ring_hops[a, d, j, step].start()

    narrow = [dko_ref, dvo_ref]
    finals = []

    def ring_end(a):
        ring_step(a, NZ // 2)
        for j in range(2):
            arriving = [incoming.at[a, d, j, hop_count(d, j) - 1] for d in range(2)]
            add_up(a, z, j, arriving, total.at[a, pl.ds(2 * j, 2)])
        mine = narrow[a].at[:, columns(x, HEAD)]
        finals.append(pltpu.make_async_copy(total.at[a, x], mine, own_fin.at[a]))
        for d in (1, 3, 2):
            to = lax.rem(x + d, NX)
            finals.append(pltpu.make_async_remote_copy(
                src_ref=total.at[a, to],
                dst_ref=mine,
                send_sem=send_fin.at[a, d - 1],
                recv_sem=recv_fin.at[a, d - 1],
                device_id=device(to, z),
                device_id_type=MESH,
            ))
        for copy in finals[-4:]:
            copy.start()

    def each(body, begin=0, end=UNITS):
        pl.loop(begin, end)(body)

    into_positions(kx, kpos)
    arrived(2)
    each(weigh, 0, 4)
    gather_step(1, 1)
    each(weigh, 4, 8)
    gather_step(1, 2)
    gather_step(1, 3)
    arrived(3)
    each(value_terms)
    ring_step(1, 0)
    gather_step(1, 4)
    into_positions(vx, vpos)
    each(attend)
    for half in range(2):
        keep(0, half).start()
    ring_step(1, 1)
    each(slope, 0, 4)
    ring_step(1, 2)
    each(slope, 4, 8)
    ring_step(0, 0)
    ring_step(1, 3)
    each(query_grad, 0, 4)
    ring_step(0, 1)
    ring_end(1)
    each(query_grad, 4, 8)
    for half in range(2):
        keep(1, half).start()
    ring_step(0, 2)
    ring_step(0, 3)
    ring_end(0)

    for row in inward:
        for copy in row[1:]:
            copy.wait_send()
    for copy in list(gather_hops.values()) + list(ring_hops.values()):
        copy.wait_send()
    for a in range(2):
        for half in range(2):
            keep(a, half).wait()

        @pl.loop(0, UNITS - 2)
        def _(i):
            outward(a, i).wait()

    for copy in finals:
        copy.wait()


def on_device(queries, keys, values, out_grad, doc_lengths, span_order):
    any_spec = pl.BlockSpec(memory_space=pl.ANY)
    smem = pl.BlockSpec(memory_space=pltpu.SMEM)
    dma = pltpu.SemaphoreType.DMA
    vmem = pltpu.VMEM
    heads = (NX, ROWS, WIDE)
    gathered = (SPANS, SPAN, HEAD)
    padded = (SPANS + REACH, SPAN, HEAD)
    windows = (UNITS, REACH + 3, SPAN, HEAD)
    stage = (UNITS, SPAN, WIDE)
    ring = (2, 2, 2, NZ // 2)
    places = jnp.arange(SPANS, dtype=jnp.int32)
    blocks = ((places // 2 % NZ) * NX + places // 2 // NZ) * 2 + places % 2
    slots = jnp.sum(jnp.where(span_order[None, :] == places[:, None], blocks[None, :], 0), axis=1)
    return pl.pallas_call(
        kernel,
        out_shape=[jax.ShapeDtypeStruct((ROWS, NX * width), BF) for width in (WIDE, WIDE, HEAD, HEAD)],
        in_specs=[smem] * 3 + [any_spec] * 4,
        out_specs=[any_spec] * 4,
        scratch_shapes=[
            vmem(heads, BF), vmem(heads, BF), vmem(gathered, BF), vmem(gathered, BF),
            vmem(padded, BF), vmem(padded, BF), vmem((UNITS, WINDOW, GROUP * SPAN), BF),
            vmem(windows, F32), vmem(windows, F32), vmem(stage, BF), vmem(stage, BF),
            vmem(ring + (2, ROWS, HEAD), BF), vmem(ring + (2, ROWS, HEAD), BF), vmem((2, NX, ROWS, HEAD), BF),
            dma((4,)), dma((4, 3)), dma((4, 3)),
            dma((2, 2)), dma((2, UNITS - 2)), dma((2, UNITS - 2)),
            dma((2,)), dma((2, 3)), dma((2, 3)),
            dma(ring), dma(ring), dma(ring), dma(ring),
        ],
        compiler_params=pltpu.CompilerParams(
            collective_id=0, has_side_effects=True, vmem_limit_bytes=56 * 2 ** 20),
        name="attention",
    )(span_order, slots, doc_lengths, queries, keys.reshape(2, SPAN, NX * HEAD), values.reshape(2, SPAN, NX * HEAD), out_grad)


def solution(mesh):
    rows = P(("grp", "seq"), None)
    return jax.shard_map(
        lambda *args: tuple(on_device(*args)),
        mesh=mesh,
        in_specs=(rows, rows, rows, rows, P("grp"), P("grp")),
        out_specs=(rows, rows, rows, rows),
        check_vma=False,
    )
```

time: 720 us -> 94.5 us (0.13); the launches traced: 709 us -> 94.2 us
  loops' own time: 200 us -> 0 us
  waiting for transfers between devices: 152 us -> 0 us
  local copies, waits for them, and re-layouts: 147 us -> 5.64 us
  matrix products: 118 us -> 0 us
  Pallas kernels: 0 us -> 87.3 us
  starting transfers between devices: 62.5 us -> 0 us
  other arithmetic: 28.8 us -> 0.64 us
    another operation x134 -> x0, loops' own time: 200 us -> none  [the longest x8 46.2 us: backward_one_block(): q_grad, k_grad, v_grad = lax.fori_loop(0, row_blk + 1, step, start)]
    all_to_all x8 -> x0, waiting for transfers between devices: 152 us -> none  [the longest x1 28.6 us: on_device(): lax.all_to_all(queries, 'seq', split_axis=1, concat_axis=0, tiled=True)]
    dot_general x112 -> x0, matrix products: 118 us -> none  [the longest x16 31.4 us: step_live(): jnp.einsum('qk,qd->kd', rounded, g_block, preferred_element_type=jnp.floa...]
    dynamic_slice x212 -> x0, local copies, waits for them, and re-layouts: 109 us -> none  [the longest x124 79.9 us: is_live(): return docs[col_blk * BLK + BLK - 1] >= docs[row_blk * BLK]]
    pallas_call x0 -> x1, Pallas kernels: none -> 87.3 us  [on_device(): pl.pallas_call(kernel, out_shape=[jax.ShapeDtypeStruct((ROWS, NX * width)...]
    all_to_all x8 -> x0, starting transfers between devices: 62.5 us -> none  [the longest x1 11.3 us: on_device(): lax.all_to_all(queries, 'seq', split_axis=1, concat_axis=0, tiled=True)]
    gather x8 -> x0, local copies, waits for them, and re-layouts: 13.9 us -> none  [the longest x4 9.08 us: into_layout(): block_tile.reshape(spans, half, block_tile.shape[1])[span_order]]
    reduce_sum x27 -> x1, other arithmetic: 14.4 us -> 0.63 us  [on_device(): jnp.sum(jnp.where(span_order[None, :] == places[:, None], blocks[None, :]...]
  transfers between devices with their start and end apart: 8 -> 0, of which waited for: 7 -> 0; matrix products, arithmetic and copies ran while one was open for 17% -> 0% of each run, Pallas kernels for 0% -> 0%
where the time goes in v2:
time: 94.5 us; the launch traced here: 94.2 us
  Pallas kernels  87.3 us (92%)
  local copies, waits for them, and re-layouts  5.64 us (6%)
    pallas_call x1, Pallas kernels, on_device(): pl.pallas_call(kernel, out_shape=[jax.ShapeDtypeStruct((ROWS, NX * width)...  87.3 us
    unnamed x12, local copies, waits for them, and re-layouts  5.64 us

profile of v2, /device:TPU:8, one launch (start us, length us, event | category | flops | bytes accessed | tf_op | source)
XLA Modules:
  0.0 94.2 jit_solution(17180624356599689072)
XLA Ops:
  0.6 0.0 copy-start.3
  0.7 0.6 copy-done.3
  1.3 0.6 select_reduce_fusion.slot_ref
  1.9 87.3 %attention.1 = (bf16[128,4096]{1,0:T(8,128)(2,1)}, bf16[128,4096]{1,0:T(8,128)(2,1)}, bf16[128,512]{1,0:T(8,128)(2,1)}, bf16[128,512]{1,0:T(8,128)(2,1)}) custom-call(s32[64]{0:T(128)} %order_ref.1, s32[64]{0:T(128)} %select_reduce_fusion.slot_ref, s32[8]{0:T(128)} %length_ref.1, bf16[128,4096]{1,0:T(8,128)(2,1)} %q_ref.1, bf16[2,64,512]{2,1,0:T(8,128)(2,1)} %bitcast.2, ...), custom_call_target="tpu_custom_call" | custom-call | tf_op jit(solution)/shard_map/attention/pallas_call | solution.py:351
  89.2 0.0 copy-start
  89.2 2.4 %copy.14 = bf16[128,4096]{1,0:T(8,128)(2,1)} copy(bf16[128,4096]{1,0:T(8,128)(2,1)} %get-tuple-element.8) | data formatting | bytes 2097152
  91.6 0.0 copy-done
  91.6 0.0 copy-start.2
  91.6 1.0 %copy.15 = bf16[128,4096]{1,0:T(8,128)(2,1)} copy(bf16[128,4096]{1,0:T(8,128)(2,1)S(1)} %copy-done) | data formatting | bytes 2097152
  92.6 0.1 copy-done.2
  92.6 0.0 copy-start.1
  92.6 0.7 copy.16
  93.3 0.3 copy-done.1
  93.6 0.7 copy.17
  (1 shorter events, 0.0 us)
Async XLA Ops:
  0.6 0.7 copy-start.3
  89.2 2.4 %copy-start = (bf16[128,4096]{1,0:T(8,128)(2,1)S(1)}, bf16[128,4096]{1,0:T(8,128)(2,1)}, u32[]{:S(2)}) copy-start(bf16[128,4096]{1,0:T(8,128)(2,1)} %get-tuple-element.9) | copy-start | bytes 3145732
  91.6 1.0 %copy-start.2 = (bf16[128,512]{1,0:T(8,128)(2,1)S(1)}, bf16[128,512]{1,0:T(8,128)(2,1)}, u32[]{:S(2)}) copy-start(bf16[128,512]{1,0:T(8,128)(2,1)} %get-tuple-element.10) | copy-start | bytes 393220
  92.6 1.0 %copy-start.1 = (bf16[128,512]{1,0:T(8,128)(2,1)S(1)}, bf16[128,512]{1,0:T(8,128)(2,1)}, u32[]{:S(2)}) copy-start(bf16[128,512]{1,0:T(8,128)(2,1)} %get-tuple-element.11) | copy-start | bytes 393220

commit v3 on v2

v3 whole, which is shorter than its diff:
```python
import math

import jax
import jax.numpy as jnp
from jax import lax
from jax.experimental import pallas as pl
from jax.experimental.pallas import tpu as pltpu
from jax.sharding import PartitionSpec as P

NX = 4
NZ = 8
ROWS = 128
SPAN = 64
HEAD = 128
GROUP = 8
WIDE = GROUP * HEAD
SPANS = 64
REACH = 16
PAD = REACH * SPAN
WINDOW = PAD + SPAN
UNITS = 2 * NX
MESH = pl.DeviceIdType.MESH
SCALE = HEAD ** -0.5
NEG = -1e30
BF = jnp.bfloat16
F32 = jnp.float32


def columns(index, width):
    return pl.ds(pl.multiple_of(index * width, width), width)


def product(a, b, contract):
    return lax.dot_general(a, b, ((contract[0], contract[1]), ((), ())), preferred_element_type=F32)


def hop_count(d, j):
    return NZ // 2 if j == d else NZ // 2 - 1


LANES = [(d, j) for j in range(2) for d in range(2)]


def kernel(order_ref, slot_ref, length_ref, q_ref, k_ref, v_ref, g_ref, oo_ref, dqo_ref, dko_ref, dvo_ref,
           qx, gx, kx, vx, kpos, vpos, probs, dkw, dvw, ost, dqst,
           outgoing, incoming, mine, total,
           own_in, send_in, recv_in, own_out, send_out, recv_out, own_fin, send_fin, recv_fin,
           gather_send, gather_recv, ring_send, ring_recv):
    me = lax.axis_index("seq")
    x, z = me // NZ, lax.rem(me, NZ)

    def device(xx, zz):
        return {"seq": lax.rem(xx + NX, NX) * NZ + lax.rem(zz + NZ, NZ)}

    barrier = pltpu.get_barrier_semaphore()
    partners = [device(x + d, z) for d in (1, 2, 3)] + [device(x, z + 1), device(x, z - 1)]
    for partner in partners:
        pl.semaphore_signal(barrier, inc=1, device_id=partner, device_id_type=MESH)
    pl.semaphore_wait(barrier, len(partners))

    sources = [k_ref, v_ref, q_ref, g_ref]
    here = pl.ds((z * NX + x) * 2, 2)
    landing = [kx.at[here], vx.at[here], qx.at[x], gx.at[x]]
    widths = [HEAD, HEAD, WIDE, WIDE]
    inward = []

    def outgoing_columns(a, to):
        return sources[a].at[:, :, columns(to, widths[a])] if a < 2 else sources[a].at[:, columns(to, widths[a])]

    for a in range(4):
        row = [pltpu.make_async_copy(outgoing_columns(a, x), landing[a], own_in.at[a])]
        for d in (1, 3, 2):
            to = lax.rem(x + d, NX)
            row.append(pltpu.make_async_remote_copy(
                src_ref=outgoing_columns(a, to),
                dst_ref=landing[a],
                send_sem=send_in.at[a, d - 1],
                recv_sem=recv_in.at[a, d - 1],
                device_id=device(to, z),
                device_id_type=MESH,
            ))
        inward.append(row)
    for a in (0, 1):
        for copy in inward[a]:
            copy.start()
    for d in range(4):
        for a in (2, 3):
            inward[a][d].start()

    def arrived(a, which=range(4)):
        for d in which:
            if d == 0:
                inward[a][0].wait()
            else:
                inward[a][d].wait_recv()

    gathered = [kx, vx]

    def gather_hop(a, d, j, step):
        sign = 1 - 2 * d
        block = gathered[a].at[pl.ds(lax.rem(z - sign * step + NZ, NZ) * 2 * NX + 4 * j, 4)]
        return pltpu.make_async_remote_copy(
            src_ref=block,
            dst_ref=block,
            send_sem=gather_send.at[a, d, j, step],
            recv_sem=gather_recv.at[a, d, j, step],
            device_id=device(x, z + sign),
            device_id_type=MESH,
        )

    def gather_step(a, step):
        for d, j in LANES:
            count = hop_count(d, j)
            if 0 < step <= count:
                gather_hop(a, d, j, step - 1).wait_recv()
            if step < count:
                gather_hop(a, d, j, step).start()

    arrived(0)
    gather_step(0, 0)
    arrived(1)
    kpos[:REACH] = jnp.zeros((REACH, SPAN, HEAD), BF)
    vpos[:REACH] = jnp.zeros((REACH, SPAN, HEAD), BF)
    for unit in range(UNITS):
        dkw[unit, 0] = jnp.zeros((SPAN, HEAD), F32)
        dkw[unit, REACH + 2] = jnp.zeros((SPAN, HEAD), F32)
        dvw[unit, 0] = jnp.zeros((SPAN, HEAD), F32)
        dvw[unit, REACH + 2] = jnp.zeros((SPAN, HEAD), F32)

    gather_step(0, 1)
    gather_step(1, 0)
    gather_step(0, 2)
    gather_step(1, 1)
    gather_step(0, 3)
    gather_step(1, 2)
    gather_step(0, 4)

    def into_positions(source, target):
        @pl.loop(0, SPANS)
        def _(p):
            target[p + REACH] = source[slot_ref[p]]

    def unit_place(i):
        t = i // 2
        return lax.rem(x + t + t // 2 - 2 * (t // 3), NX), lax.rem(i, 2)

    def unit_span(i):
        xx, half = unit_place(i)
        return order_ref[2 * (xx * NZ + z) + half]

    def window(ref, i):
        c = unit_span(i)
        return jnp.concatenate([ref[c + j] for j in range(REACH + 1)], axis=0)

    def stacked(ref, i):
        xx, half = unit_place(i)
        rows = pl.ds(pl.multiple_of(half * SPAN, SPAN), SPAN)
        return jnp.concatenate([ref[xx, rows, h * HEAD:(h + 1) * HEAD] for h in range(GROUP)], axis=0)

    starts = []
    running = length_ref[0]
    for i in range(1, 8):
        starts.append(running)
        running = running + length_ref[i]

    def weigh(i):
        c = unit_span(i)
        row = c * SPAN + lax.rem(lax.broadcasted_iota(jnp.int32, (1, HEAD), 1), SPAN)
        first = jnp.zeros((1, HEAD), jnp.int32)
        for start in starts:
            first = jnp.where(row >= start, start, first)
        key = (c - REACH) * SPAN + lax.broadcasted_iota(jnp.int32, (WINDOW, HEAD), 0)
        seen = (key >= first) & (key <= row)
        scores = product(window(kpos, i), stacked(qx, i), ((1,), (1,)))
        scores = jnp.where(jnp.concatenate([seen] * (GROUP // 2), axis=1), scores * (SCALE * math.log2(math.e)), NEG)
        weights = jnp.exp2(scores - jnp.max(scores, axis=0, keepdims=True))
        p = (weights * (1.0 / jnp.sum(weights, axis=0, keepdims=True))).astype(BF)
        probs[i] = p
        dvw[i, 1:REACH + 2] = jnp.dot(
            p, stacked(gx, i), preferred_element_type=F32).reshape(REACH + 1, SPAN, HEAD)

    def put_heads(target, i, value_t):
        value = value_t.T
        for h in range(GROUP):
            target[i, :, h * HEAD:(h + 1) * HEAD] = value[h * SPAN:(h + 1) * SPAN]

    staged = [ost, dqst]
    results = [oo_ref, dqo_ref]

    def outward(a, i):
        xx, half = unit_place(i)
        rows = pl.ds(pl.multiple_of(half * SPAN, SPAN), SPAN)
        return pltpu.make_async_remote_copy(
            src_ref=staged[a].at[i],
            dst_ref=results[a].at[rows, columns(x, WIDE)],
            send_sem=send_out.at[a, i - 2],
            recv_sem=recv_out.at[a, i - 2],
            device_id=device(xx, z),
            device_id_type=MESH,
        )

    def keep(a, half):
        rows = pl.ds(half * SPAN, SPAN)
        return pltpu.make_async_copy(
            staged[a].at[half], results[a].at[rows, columns(x, WIDE)], own_out.at[a, half])

    def attend(i):
        q, g, p = stacked(qx, i), stacked(gx, i), probs[i]
        k, v = window(kpos, i), window(vpos, i)
        o_t = product(v, p, ((0,), (0,))).astype(BF)
        delta = jnp.sum(o_t.astype(F32) * g.T.astype(F32), axis=0, keepdims=True)
        slopes = (p.astype(F32) * (product(v, g, ((1,), (1,))) - delta)).astype(BF)
        dkw[i, 1:REACH + 2] = jnp.dot(
            slopes, q, preferred_element_type=F32).reshape(REACH + 1, SPAN, HEAD)
        put_heads(ost, i, o_t)
        put_heads(dqst, i, (product(k, slopes, ((0,), (0,))) * SCALE).astype(BF))

    terms = [dkw, dvw]
    factors = [SCALE, 1.0]

    def ring_hop(a, d, j, step):
        return pltpu.make_async_remote_copy(
            src_ref=outgoing.at[a, d, j, step],
            dst_ref=incoming.at[a, d, j, step],
            send_sem=ring_send.at[a, d, j, step],
            recv_sem=ring_recv.at[a, d, j, step],
            device_id=device(x, z + 1 - 2 * d),
            device_id_type=MESH,
        )

    def own_terms(a, block, j, target):
        spans = [unit_span(i) for i in range(UNITS)]

        @pl.loop(0, 4)
        def _(u):
            position = order_ref[2 * ((2 * j + u // 2) * NZ + block) + lax.rem(u, 2)]
            value = jnp.zeros((SPAN, HEAD), F32)
            for i in range(UNITS):
                away = jnp.clip(position - spans[i] + REACH + 1, 0, REACH + 2)
                value += terms[a][i, away]
            target[u] = value * factors[a]

    def ring_step(a, step):
        lanes = [(d, j) for d, j in LANES if step < hop_count(d, j)]

        def prepare(d, j):
            sign = 1 - 2 * d
            own_terms(a, lax.rem(z + sign * (hop_count(d, j) - step) + NZ, NZ), j, mine.at[d, j])

        if step > 0:
            for d, j in lanes:
                prepare(d, j)
        for d, j in lanes:
            if step == 0:
                prepare(d, j)
            value = mine[d, j]
            if step > 0:
                ring_hop(a, d, j, step - 1).wait_recv()
                value += incoming[a, d, j, step - 1].astype(F32)
            outgoing[a, d, j, step] = value.astype(BF)
            ring_hop(a, d, j, step).start()

    narrow = [dko_ref, dvo_ref]
    finals = []

    def ring_end(a):
        for j in range(2):
            own_terms(a, z, j, mine.at[0, j])
        for j in range(2):
            value = mine[0, j]
            for d in range(2):
                last = hop_count(d, j) - 1
                ring_hop(a, d, j, last).wait_recv()
                value += incoming[a, d, j, last].astype(F32)
            total[a, 4 * j:4 * j + 4] = value.astype(BF)
        place = narrow[a].at[:, :, columns(x, HEAD)]
        finals.append(pltpu.make_async_copy(total.at[a, pl.ds(2 * x, 2)], place, own_fin.at[a]))
        for d in (1, 3, 2):
            to = lax.rem(x + d, NX)
            finals.append(pltpu.make_async_remote_copy(
                src_ref=total.at[a, pl.ds(2 * to, 2)],
                dst_ref=place,
                send_sem=send_fin.at[a, d - 1],
                recv_sem=recv_fin.at[a, d - 1],
                device_id=device(to, z),
                device_id_type=MESH,
            ))
        for copy in finals[-4:]:
            copy.start()

    into_positions(kx, kpos)

    @pl.loop(0, NX)
    def _(t):
        for k, source in enumerate((0, 2, 1, 3)):
            @pl.when(t == k)
            def _(k=k, source=source):
                arrived(2, (source,))
                arrived(3, (source,))
                if k == 2:
                    gather_step(1, 3)

        weigh(2 * t)
        weigh(2 * t + 1)

    ring_step(1, 0)
    gather_step(1, 4)
    into_positions(vx, vpos)

    @pl.loop(0, NX)
    def _(k):
        t = NX - 1 - k
        for step in (1, 2):
            pl.when(k == step)(lambda step=step: ring_step(1, step))
        attend(2 * t)
        attend(2 * t + 1)

        @pl.when(t > 0)
        def _():
            for half in range(2):
                for a in range(2):
                    outward(a, 2 * t + half).start()

    for a in range(2):
        for half in range(2):
            keep(a, half).start()
    ring_step(0, 0)
    ring_step(1, 3)
    ring_step(0, 1)
    ring_end(1)
    ring_step(0, 2)
    ring_step(0, 3)
    ring_end(0)

    for row in inward:
        for copy in row[1:]:
            copy.wait_send()
    for a in range(2):
        for d, j in LANES:
            for step in range(hop_count(d, j)):
                gather_hop(a, d, j, step).wait_send()
                ring_hop(a, d, j, step).wait_send()
    for a in range(2):
        for half in range(2):
            keep(a, half).wait()

        @pl.loop(2, UNITS)
        def _(i):
            outward(a, i).wait()

    for copy in finals:
        copy.wait()


def on_device(queries, keys, values, out_grad, doc_lengths, span_order):
    any_spec = pl.BlockSpec(memory_space=pl.ANY)
    smem = pl.BlockSpec(memory_space=pltpu.SMEM)
    dma = pltpu.SemaphoreType.DMA
    vmem = pltpu.VMEM
    heads = (NX, ROWS, WIDE)
    gathered = (SPANS, SPAN, HEAD)
    padded = (SPANS + REACH, SPAN, HEAD)
    windows = (UNITS, REACH + 3, SPAN, HEAD)
    stage = (UNITS, SPAN, WIDE)
    ring = (2, 2, 2, NZ // 2)
    piece = (4, SPAN, HEAD)
    places = jnp.arange(SPANS, dtype=jnp.int32)
    blocks = ((places // 2 % NZ) * NX + places // 2 // NZ) * 2 + places % 2
    slots = jnp.sum(jnp.where(span_order[None, :] == places[:, None], blocks[None, :], 0), axis=1)
    attended, grad_q, grad_k, grad_v = pl.pallas_call(
        kernel,
        out_shape=[jax.ShapeDtypeStruct((ROWS, NX * WIDE), BF)] * 2 + [
            jax.ShapeDtypeStruct((2, SPAN, NX * HEAD), BF)] * 2,
        in_specs=[smem] * 3 + [any_spec] * 4,
        out_specs=[any_spec] * 4,
        scratch_shapes=[
            vmem(heads, BF), vmem(heads, BF), vmem(gathered, BF), vmem(gathered, BF),
            vmem(padded, BF), vmem(padded, BF), vmem((UNITS, WINDOW, GROUP * SPAN), BF),
            vmem(windows, F32), vmem(windows, F32), vmem(stage, BF), vmem(stage, BF),
            vmem(ring + piece, BF), vmem(ring + piece, BF), vmem((2, 2) + piece, F32), vmem((2, UNITS, SPAN, HEAD), BF),
            dma((4,)), dma((4, 3)), dma((4, 3)),
            dma((2, 2)), dma((2, UNITS - 2)), dma((2, UNITS - 2)),
            dma((2,)), dma((2, 3)), dma((2, 3)),
            dma(ring), dma(ring), dma(ring), dma(ring),
        ],
        compiler_params=pltpu.CompilerParams(
            collective_id=0, has_side_effects=True, vmem_limit_bytes=56 * 2 ** 20),
        name="attention",
    )(span_order, slots, doc_lengths, queries, keys.reshape(2, SPAN, NX * HEAD), values.reshape(2, SPAN, NX * HEAD), out_grad)
    return attended, grad_q, grad_k.reshape(ROWS, NX * HEAD), grad_v.reshape(ROWS, NX * HEAD)


def solution(mesh):
    rows = P(("grp", "seq"), None)
    return jax.shard_map(
        on_device,
        mesh=mesh,
        in_specs=(rows, rows, rows, rows, P("grp"), P("grp")),
        out_specs=(rows, rows, rows, rows),
        check_vma=False,
    )
```

time: 94.5 us -> 83.8 us (0.89)
  Pallas kernels: 87.3 us -> 76.7 us
    pallas_call x1, Pallas kernels: 87.3 us -> 76.7 us  [on_device(): pl.pallas_call(kernel, out_shape=[jax.ShapeDtypeStruct((ROWS, NX * WIDE),...]
where the time goes in v3:
time: 83.8 us; the launch traced here: 83.6 us
  Pallas kernels  76.7 us (92%)
  local copies, waits for them, and re-layouts  5.64 us (7%)
    pallas_call x1, Pallas kernels, on_device(): pl.pallas_call(kernel, out_shape=[jax.ShapeDtypeStruct((ROWS, NX * WIDE),...  76.7 us
    unnamed x12, local copies, waits for them, and re-layouts  5.64 us

profile of v3, /device:TPU:8, one launch (start us, length us, event | category | flops | bytes accessed | tf_op | source)
XLA Modules:
  0.0 83.6 jit_solution(6033586060196578391)
XLA Ops:
  0.6 0.0 copy-start.3
  0.7 0.6 copy-done.3
  1.3 0.6 select_reduce_fusion.slot_ref
  1.9 76.7 %attention.1 = (bf16[128,4096]{1,0:T(8,128)(2,1)}, bf16[128,4096]{1,0:T(8,128)(2,1)}, bf16[2,64,512]{2,1,0:T(8,128)(2,1)}, bf16[2,64,512]{2,1,0:T(8,128)(2,1)}) custom-call(s32[64]{0:T(128)} %order_ref.1, s32[64]{0:T(128)} %select_reduce_fusion.slot_ref, s32[8]{0:T(128)} %length_ref.1, bf16[128,4096]{1,0:T(8,128)(2,1)} %q_ref.1, ...), custom_call_target="tpu_custom_call" | custom-call | tf_op jit(solution)/shard_map/attention/pallas_call | solution.py:370
  78.6 0.0 copy-start
  78.6 2.4 %copy.14 = bf16[128,4096]{1,0:T(8,128)(2,1)} copy(bf16[128,4096]{1,0:T(8,128)(2,1)} %get-tuple-element.16) | data formatting | bytes 2097152
  81.0 0.0 copy-done
  81.0 0.0 copy-start.2
  81.0 1.0 %copy.15 = bf16[128,4096]{1,0:T(8,128)(2,1)} copy(bf16[128,4096]{1,0:T(8,128)(2,1)S(1)} %copy-done) | data formatting | bytes 2097152
  82.0 0.1 copy-done.2
  82.0 0.0 copy-start.1
  82.0 0.7 copy.16
  82.7 0.3 copy-done.1
  83.0 0.7 copy.17
  (1 shorter events, 0.0 us)
Async XLA Ops:
  0.6 0.7 copy-start.3
  78.6 2.4 %copy-start = (bf16[128,4096]{1,0:T(8,128)(2,1)S(1)}, bf16[128,4096]{1,0:T(8,128)(2,1)}, u32[]{:S(2)}) copy-start(bf16[128,4096]{1,0:T(8,128)(2,1)} %get-tuple-element.17) | copy-start | bytes 3145732
  81.0 1.0 %copy-start.2 = (bf16[2,64,512]{2,1,0:T(8,128)(2,1)S(1)}, bf16[2,64,512]{2,1,0:T(8,128)(2,1)}, u32[]{:S(2)}) copy-start(bf16[2,64,512]{2,1,0:T(8,128)(2,1)} %get-tuple-element.10) | copy-start | bytes 393220
  82.0 1.0 %copy-start.1 = (bf16[2,64,512]{2,1,0:T(8,128)(2,1)S(1)}, bf16[2,64,512]{2,1,0:T(8,128)(2,1)}, u32[]{:S(2)}) copy-start(bf16[2,64,512]{2,1,0:T(8,128)(2,1)} %get-tuple-element.11) | copy-start | bytes 393220

commit v4 on v3

--- a/solution.py
+++ b/solution.py
@@ -38,13 +38,13 @@
     return NZ // 2 if j == d else NZ // 2 - 1
 
 
-LANES = [(d, j) for j in range(2) for d in range(2)]
-
-
-def kernel(order_ref, slot_ref, length_ref, q_ref, k_ref, v_ref, g_ref, oo_ref, dqo_ref, dko_ref, dvo_ref,
-           qx, gx, kx, vx, kpos, vpos, probs, dkw, dvw, ost, dqst,
+LANES = [(0, 0), (1, 1), (0, 1), (1, 0)]
+
+
+def kernel(order_ref, length_ref, q_ref, k_ref, v_ref, g_ref, oo_ref, dqo_ref, dko_ref, dvo_ref,
+           qx, gx, kx, vx, kpos, vpos, probs, dkw, dvw, ost, dqst, slot_v, slot_ref,
            outgoing, incoming, mine, total,
-           own_in, send_in, recv_in, own_out, send_out, recv_out, own_fin, send_fin, recv_fin,
+           slot_sem, own_in, send_in, recv_in, own_out, send_out, recv_out, own_fin, send_fin, recv_fin,
            gather_send, gather_recv, ring_send, ring_recv):
     me = lax.axis_index("seq")
     x, z = me // NZ, lax.rem(me, NZ)
@@ -119,6 +119,35 @@
     arrived(0)
     gather_step(0, 0)
     arrived(1)
+    def unit_place(i):
+        pair, side = i // 2, lax.rem(i, 2)
+        near = (pair + 1) // 2 - 2 * (pair // 3)
+        away = near * (1 + 2 * side) + 2 * (pair // 3)
+        return lax.rem(x + away, NX), near * (pair - 1) + (1 - near) * side
+
+    def unit_span(i):
+        xx, half = unit_place(i)
+        return order_ref[2 * (xx * NZ + z) + half]
+
+    lane = lax.broadcasted_iota(jnp.int32, (UNITS, HEAD), 1)
+    line = lax.broadcasted_iota(jnp.int32, (UNITS, HEAD), 0)
+
+    def find(t, found):
+        block = (lax.rem(t // 2, NZ) * NX + t // (2 * NZ)) * 2 + lax.rem(t, 2)
+        position = order_ref[t]
+        return jnp.where(lane == position, block, found[0]), jnp.where(lane == block, position, found[1])
+
+    nothing = jnp.zeros((UNITS, HEAD), jnp.int32)
+    blocks, positions = lax.fori_loop(0, SPANS, find, (nothing, nothing))
+    for i in range(UNITS):
+        nothing = jnp.where(line == i, unit_span(i), nothing)
+    slot_v[0] = blocks
+    slot_v[1] = jnp.clip(positions - nothing + REACH + 1, 0, REACH + 2)
+    pltpu.make_async_copy(slot_v, slot_ref, slot_sem.at[0]).start()
+
+    def wait_slots():
+        pltpu.make_async_copy(slot_v, slot_ref, slot_sem.at[0]).wait()
+
     kpos[:REACH] = jnp.zeros((REACH, SPAN, HEAD), BF)
     vpos[:REACH] = jnp.zeros((REACH, SPAN, HEAD), BF)
     for unit in range(UNITS):
@@ -138,15 +167,7 @@
     def into_positions(source, target):
         @pl.loop(0, SPANS)
         def _(p):
-            target[p + REACH] = source[slot_ref[p]]
-
-    def unit_place(i):
-        t = i // 2
-        return lax.rem(x + t + t // 2 - 2 * (t // 3), NX), lax.rem(i, 2)
-
-    def unit_span(i):
-        xx, half = unit_place(i)
-        return order_ref[2 * (xx * NZ + z) + half]
+            target[p + REACH] = source[slot_ref[0, 0, p]]
 
     def window(ref, i):
         c = unit_span(i)
@@ -229,15 +250,11 @@
         )
 
     def own_terms(a, block, j, target):
-        spans = [unit_span(i) for i in range(UNITS)]
-
         @pl.loop(0, 4)
         def _(u):
-            position = order_ref[2 * ((2 * j + u // 2) * NZ + block) + lax.rem(u, 2)]
             value = jnp.zeros((SPAN, HEAD), F32)
             for i in range(UNITS):
-                away = jnp.clip(position - spans[i] + REACH + 1, 0, REACH + 2)
-                value += terms[a][i, away]
+                value += terms[a][i, slot_ref[1, i, block * 2 * NX + 4 * j + u]]
             target[u] = value * factors[a]
 
     def ring_step(a, step):
@@ -263,45 +280,66 @@
     narrow = [dko_ref, dvo_ref]
     finals = []
 
+    def final(a, to, d):
+        return pltpu.make_async_remote_copy(
+            src_ref=total.at[a, pl.ds(2 * to, 2)],
+            dst_ref=narrow[a].at[:, :, columns(x, HEAD)],
+            send_sem=send_fin.at[a, d],
+            recv_sem=recv_fin.at[a, d],
+            device_id=device(to, z),
+            device_id_type=MESH,
+        )
+
+    def final_own(a):
+        return pltpu.make_async_copy(
+            total.at[a, pl.ds(2 * x, 2)], narrow[a].at[:, :, columns(x, HEAD)], own_fin.at[a])
+
     def ring_end(a):
         for j in range(2):
             own_terms(a, z, j, mine.at[0, j])
         for j in range(2):
             value = mine[0, j]
-            for d in range(2):
+            for d in (1 - j, j):
                 last = hop_count(d, j) - 1
                 ring_hop(a, d, j, last).wait_recv()
                 value += incoming[a, d, j, last].astype(F32)
             total[a, 4 * j:4 * j + 4] = value.astype(BF)
-        place = narrow[a].at[:, :, columns(x, HEAD)]
-        finals.append(pltpu.make_async_copy(total.at[a, pl.ds(2 * x, 2)], place, own_fin.at[a]))
-        for d in (1, 3, 2):
-            to = lax.rem(x + d, NX)
-            finals.append(pltpu.make_async_remote_copy(
-                src_ref=total.at[a, pl.ds(2 * to, 2)],
-                dst_ref=place,
-                send_sem=send_fin.at[a, d - 1],
-                recv_sem=recv_fin.at[a, d - 1],
-                device_id=device(to, z),
-                device_id_type=MESH,
-            ))
-        for copy in finals[-4:]:
-            copy.start()
-
+            for d in (2, 1, 3):
+                to = lax.rem(x + d, NX)
+                pl.when(to // 2 == j)(lambda to=to, d=d: final(a, to, d - 1).start())
+            pl.when(x // 2 == j)(lambda: final_own(a).start())
+
+    def take_in(k):
+        source = (0, 2, 1, 3)[k]
+        arrived(2, (source,))
+        arrived(3, (source,))
+
+    def attend_pair(t):
+        attend(2 * t)
+        attend(2 * t + 1)
+
+    def send_pair(t):
+        for half in range(2):
+            for a in range(2):
+                outward(a, 2 * t + half).start()
+
+    wait_slots()
     into_positions(kx, kpos)
 
-    @pl.loop(0, NX)
+    @pl.loop(0, 2)
     def _(t):
-        for k, source in enumerate((0, 2, 1, 3)):
-            @pl.when(t == k)
-            def _(k=k, source=source):
-                arrived(2, (source,))
-                arrived(3, (source,))
-                if k == 2:
-                    gather_step(1, 3)
-
-        weigh(2 * t)
-        weigh(2 * t + 1)
+        @pl.when(t == 0)
+        def _():
+            for k in range(3):
+                take_in(k)
+
+        @pl.when(t == 1)
+        def _():
+            gather_step(1, 3)
+            take_in(3)
+
+        for k in range(4):
+            weigh(4 * t + k)
 
     ring_step(1, 0)
     gather_step(1, 4)
@@ -309,17 +347,11 @@
 
     @pl.loop(0, NX)
     def _(k):
-        t = NX - 1 - k
+        pair = 1 + 2 * k - 3 * (k // 2) - 4 * (k // 3)
         for step in (1, 2):
             pl.when(k == step)(lambda step=step: ring_step(1, step))
-        attend(2 * t)
-        attend(2 * t + 1)
-
-        @pl.when(t > 0)
-        def _():
-            for half in range(2):
-                for a in range(2):
-                    outward(a, 2 * t + half).start()
+        attend_pair(pair)
+        pl.when(k < 3)(lambda: send_pair(pair))
 
     for a in range(2):
         for half in range(2):
@@ -348,8 +380,34 @@
         def _(i):
             outward(a, i).wait()
 
-    for copy in finals:
-        copy.wait()
+    for a in range(2):
+        final_own(a).wait()
+        for d in (1, 2, 3):
+            final(a, lax.rem(x + d, NX), d - 1).wait()
+
+
+def hand_over(*refs):
+    sources, targets, held = refs[:4], refs[4:8], refs[8:12]
+    sem_in, sem_out = refs[12:]
+    pieces = [(a, k) for a in range(4) for k in range(4 if a < 2 else 1)]
+
+    def part(ref, a, k):
+        size = ROWS // (4 if a < 2 else 1)
+        return ref[a].at[pl.ds(k * size, size)]
+
+    def bring(a, k):
+        return pltpu.make_async_copy(part(sources, a, k), part(held, a, k), sem_in.at[a, k])
+
+    def give(a, k):
+        return pltpu.make_async_copy(part(held, a, k), part(targets, a, k), sem_out.at[a, k])
+
+    for piece in pieces:
+        bring(*piece).start()
+    for piece in pieces:
+        bring(*piece).wait()
+        give(*piece).start()
+    for piece in pieces:
+        give(*piece).wait()
 
 
 def on_device(queries, keys, values, out_grad, doc_lengths, span_order):
@@ -364,21 +422,19 @@
     stage = (UNITS, SPAN, WIDE)
     ring = (2, 2, 2, NZ // 2)
     piece = (4, SPAN, HEAD)
-    places = jnp.arange(SPANS, dtype=jnp.int32)
-    blocks = ((places // 2 % NZ) * NX + places // 2 // NZ) * 2 + places % 2
-    slots = jnp.sum(jnp.where(span_order[None, :] == places[:, None], blocks[None, :], 0), axis=1)
     attended, grad_q, grad_k, grad_v = pl.pallas_call(
         kernel,
         out_shape=[jax.ShapeDtypeStruct((ROWS, NX * WIDE), BF)] * 2 + [
             jax.ShapeDtypeStruct((2, SPAN, NX * HEAD), BF)] * 2,
-        in_specs=[smem] * 3 + [any_spec] * 4,
+        in_specs=[smem] * 2 + [any_spec] * 4,
         out_specs=[any_spec] * 4,
         scratch_shapes=[
             vmem(heads, BF), vmem(heads, BF), vmem(gathered, BF), vmem(gathered, BF),
             vmem(padded, BF), vmem(padded, BF), vmem((UNITS, WINDOW, GROUP * SPAN), BF),
             vmem(windows, F32), vmem(windows, F32), vmem(stage, BF), vmem(stage, BF),
+            vmem((2, UNITS, HEAD), jnp.int32), pltpu.SMEM((2, UNITS, HEAD), jnp.int32),
             vmem(ring + piece, BF), vmem(ring + piece, BF), vmem((2, 2) + piece, F32), vmem((2, UNITS, SPAN, HEAD), BF),
-            dma((4,)), dma((4, 3)), dma((4, 3)),
+            dma((1,)), dma((4,)), dma((4, 3)), dma((4, 3)),
             dma((2, 2)), dma((2, UNITS - 2)), dma((2, UNITS - 2)),
             dma((2,)), dma((2, 3)), dma((2, 3)),
             dma(ring), dma(ring), dma(ring), dma(ring),
@@ -386,14 +442,22 @@
         compiler_params=pltpu.CompilerParams(
             collective_id=0, has_side_effects=True, vmem_limit_bytes=56 * 2 ** 20),
         name="attention",
-    )(span_order, slots, doc_lengths, queries, keys.reshape(2, SPAN, NX * HEAD), values.reshape(2, SPAN, NX * HEAD), out_grad)
-    return attended, grad_q, grad_k.reshape(ROWS, NX * HEAD), grad_v.reshape(ROWS, NX * HEAD)
+    )(span_order, doc_lengths, queries, keys.reshape(2, SPAN, NX * HEAD), values.reshape(2, SPAN, NX * HEAD), out_grad)
+    results = (attended, grad_q, grad_k.reshape(ROWS, NX * HEAD), grad_v.reshape(ROWS, NX * HEAD))
+    return pl.pallas_call(
+        hand_over,
+        out_shape=[jax.ShapeDtypeStruct(result.shape, BF) for result in results],
+        in_specs=[any_spec] * 4,
+        out_specs=[any_spec] * 4,
+        scratch_shapes=[vmem(result.shape, BF) for result in results] + [dma((4, 4)), dma((4, 4))],
+        name="hand_over",
+    )(*results)
 
 
 def solution(mesh):
     rows = P(("grp", "seq"), None)
     return jax.shard_map(
-        on_device,
+        lambda *args: tuple(on_device(*args)),
         mesh=mesh,
         in_specs=(rows, rows, rows, rows, P("grp"), P("grp")),
         out_specs=(rows, rows, rows, rows),

time: 83.8 us -> 78.3 us (0.934)
  local copies, waits for them, and re-layouts: 5.64 us -> 0 us
    unnamed x12 -> x0, local copies, waits for them, and re-layouts: 5.64 us -> none
    pallas_call x0 -> x1, Pallas kernels: none -> 2.62 us  [on_device(): pl.pallas_call(hand_over, out_shape=[jax.ShapeDtypeStruct(result.shape, B...]
    pallas_call x1, Pallas kernels: 76.7 us -> 74.9 us  [on_device(): pl.pallas_call(kernel, out_shape=[jax.ShapeDtypeStruct((ROWS, NX * WIDE),...]
where the time goes in v4:
time: 78.3 us; the launch traced here: 78.2 us
  Pallas kernels  77.5 us (99%)
    pallas_call x1, Pallas kernels, on_device(): pl.pallas_call(kernel, out_shape=[jax.ShapeDtypeStruct((ROWS, NX * WIDE),...  74.9 us
    pallas_call x1, Pallas kernels, on_device(): pl.pallas_call(hand_over, out_shape=[jax.ShapeDtypeStruct(result.shape, B...  2.62 us

profile of v4, /device:TPU:8, one launch (start us, length us, event | category | flops | bytes accessed | tf_op | source)
XLA Modules:
  0.0 78.2 jit_solution(2782336628885163194)
XLA Ops:
  0.6 74.9 %attention.1 = (bf16[128,4096]{1,0:T(8,128)(2,1)}, bf16[128,4096]{1,0:T(8,128)(2,1)}, bf16[2,64,512]{2,1,0:T(8,128)(2,1)}, bf16[2,64,512]{2,1,0:T(8,128)(2,1)}) custom-call(s32[64]{0:T(128)} %order_ref.1, s32[8]{0:T(128)} %length_ref.1, bf16[128,4096]{1,0:T(8,128)(2,1)} %q_ref.1, bf16[2,64,512]{2,1,0:T(8,128)(2,1)} %bitcast.4, bf16[2,64,512]{2,1,0:T(8,128)(2,1)} %bitcast.5, ...), custom_call_target="tpu_custom_call" | custom-call | tf_op jit(solution)/shard_map/attention/pallas_call | solution.py:425
  75.6 2.6 %hand_over.1 = (bf16[128,4096]{1,0:T(8,128)(2,1)}, bf16[128,4096]{1,0:T(8,128)(2,1)}, bf16[128,512]{1,0:T(8,128)(2,1)}, bf16[128,512]{1,0:T(8,128)(2,1)}) custom-call(bf16[128,4096]{1,0:T(8,128)(2,1)} %get-tuple-element.8.refs_0_, bf16[128,4096]{1,0:T(8,128)(2,1)} %get-tuple-element.9.refs_1_, bf16[128,512]{1,0:T(8,128)(2,1)} %bitcast.6, ...), custom_call_target="tpu_custom_call" | custom-call | tf_op jit(solution)/shard_map/hand_over/pallas_call | solution.py:447

commit v5 on v4

--- a/solution.py
+++ b/solution.py
@@ -227,14 +227,17 @@
 
     def attend(i):
         q, g, p = stacked(qx, i), stacked(gx, i), probs[i]
-        k, v = window(kpos, i), window(vpos, i)
+        v = window(vpos, i)
         o_t = product(v, p, ((0,), (0,))).astype(BF)
         delta = jnp.sum(o_t.astype(F32) * g.T.astype(F32), axis=0, keepdims=True)
         slopes = (p.astype(F32) * (product(v, g, ((1,), (1,))) - delta)).astype(BF)
         dkw[i, 1:REACH + 2] = jnp.dot(
             slopes, q, preferred_element_type=F32).reshape(REACH + 1, SPAN, HEAD)
+        probs[i] = slopes
         put_heads(ost, i, o_t)
-        put_heads(dqst, i, (product(k, slopes, ((0,), (0,))) * SCALE).astype(BF))
+
+    def query_grad(i):
+        put_heads(dqst, i, (product(window(kpos, i), probs[i], ((0,), (0,))) * SCALE).astype(BF))
 
     terms = [dkw, dvw]
     factors = [SCALE, 1.0]
@@ -314,14 +317,19 @@
         arrived(2, (source,))
         arrived(3, (source,))
 
-    def attend_pair(t):
-        attend(2 * t)
-        attend(2 * t + 1)
-
-    def send_pair(t):
-        for half in range(2):
-            for a in range(2):
-                outward(a, 2 * t + half).start()
+    def each_pair(a, body, begin, end, beside=None):
+        @pl.loop(begin, end)
+        def _(k):
+            pair = 1 + 2 * k - 3 * (k // 2) - 4 * (k // 3)
+            if beside is not None:
+                beside(k)
+            body(2 * pair)
+            body(2 * pair + 1)
+
+            @pl.when(k < 3)
+            def _():
+                for side in range(2):
+                    outward(a, 2 * pair + side).start()
 
     wait_slots()
     into_positions(kx, kpos)
@@ -345,20 +353,21 @@
     gather_step(1, 4)
     into_positions(vx, vpos)
 
-    @pl.loop(0, NX)
-    def _(k):
-        pair = 1 + 2 * k - 3 * (k // 2) - 4 * (k // 3)
-        for step in (1, 2):
-            pl.when(k == step)(lambda step=step: ring_step(1, step))
-        attend_pair(pair)
-        pl.when(k < 3)(lambda: send_pair(pair))
-
+    def beside(k):
+        pl.when(k == 1)(lambda: ring_step(1, 1))
+        pl.when(k == 3)(lambda: ring_step(1, 2))
+
+    each_pair(0, attend, 0, 4, beside)
+    ring_step(0, 0)
+
+    def beside_query(k):
+        pl.when(k == 1)(lambda: ring_step(1, 3))
+        pl.when(k == 3)(lambda: ring_step(0, 1))
+
+    each_pair(1, query_grad, 0, 4, beside_query)
     for a in range(2):
         for half in range(2):
             keep(a, half).start()
-    ring_step(0, 0)
-    ring_step(1, 3)
-    ring_step(0, 1)
     ring_end(1)
     ring_step(0, 2)
     ring_step(0, 3)

time: 78.3 us -> 76.9 us (0.982)
  Pallas kernels: 77.5 us -> 76.1 us
    pallas_call x1, Pallas kernels: 74.9 us -> 73.5 us  [on_device(): pl.pallas_call(kernel, out_shape=[jax.ShapeDtypeStruct((ROWS, NX * WIDE),...]
where the time goes in v5:
time: 76.9 us; the launch traced here: 76.7 us
  Pallas kernels  76.1 us (99%)
    pallas_call x1, Pallas kernels, on_device(): pl.pallas_call(kernel, out_shape=[jax.ShapeDtypeStruct((ROWS, NX * WIDE),...  73.5 us
    pallas_call x1, Pallas kernels, on_device(): pl.pallas_call(hand_over, out_shape=[jax.ShapeDtypeStruct(result.shape, B...  2.62 us

profile of v5, /device:TPU:8, one launch (start us, length us, event | category | flops | bytes accessed | tf_op | source)
XLA Modules:
  0.0 76.7 jit_solution(5275239197925780074)
XLA Ops:
  0.6 73.5 %attention.1 = (bf16[128,4096]{1,0:T(8,128)(2,1)}, bf16[128,4096]{1,0:T(8,128)(2,1)}, bf16[2,64,512]{2,1,0:T(8,128)(2,1)}, bf16[2,64,512]{2,1,0:T(8,128)(2,1)}) custom-call(s32[64]{0:T(128)} %order_ref.1, s32[8]{0:T(128)} %length_ref.1, bf16[128,4096]{1,0:T(8,128)(2,1)} %q_ref.1, bf16[2,64,512]{2,1,0:T(8,128)(2,1)} %bitcast.4, bf16[2,64,512]{2,1,0:T(8,128)(2,1)} %bitcast.5, ...), custom_call_target="tpu_custom_call" | custom-call | tf_op jit(solution)/shard_map/attention/pallas_call | solution.py:434
  74.1 2.6 %hand_over.1 = (bf16[128,4096]{1,0:T(8,128)(2,1)}, bf16[128,4096]{1,0:T(8,128)(2,1)}, bf16[128,512]{1,0:T(8,128)(2,1)}, bf16[128,512]{1,0:T(8,128)(2,1)}) custom-call(bf16[128,4096]{1,0:T(8,128)(2,1)} %get-tuple-element.8.refs_0_, bf16[128,4096]{1,0:T(8,128)(2,1)} %get-tuple-element.9.refs_1_, bf16[128,512]{1,0:T(8,128)(2,1)} %bitcast.6, ...), custom_call_target="tpu_custom_call" | custom-call | tf_op jit(solution)/shard_map/hand_over/pallas_call | solution.py:456

commit v6 on v5

--- a/solution.py
+++ b/solution.py
@@ -116,9 +116,6 @@
             if step < count:
                 gather_hop(a, d, j, step).start()
 
-    arrived(0)
-    gather_step(0, 0)
-    arrived(1)
     def unit_place(i):
         pair, side = i // 2, lax.rem(i, 2)
         near = (pair + 1) // 2 - 2 * (pair // 3)
@@ -156,7 +153,10 @@
         dvw[unit, 0] = jnp.zeros((SPAN, HEAD), F32)
         dvw[unit, REACH + 2] = jnp.zeros((SPAN, HEAD), F32)
 
+    arrived(0)
+    gather_step(0, 0)
     gather_step(0, 1)
+    arrived(1)
     gather_step(1, 0)
     gather_step(0, 2)
     gather_step(1, 1)

time: 76.9 us -> 76.9 us (level)
  no operation moved by 1% of the time
where the time goes in v6:
time: 76.9 us; the launch traced here: 76.8 us
  Pallas kernels  76.1 us (99%)
    pallas_call x1, Pallas kernels, on_device(): pl.pallas_call(kernel, out_shape=[jax.ShapeDtypeStruct((ROWS, NX * WIDE),...  73.5 us
    pallas_call x1, Pallas kernels, on_device(): pl.pallas_call(hand_over, out_shape=[jax.ShapeDtypeStruct(result.shape, B...  2.62 us

profile of v6, /device:TPU:8, one launch (start us, length us, event | category | flops | bytes accessed | tf_op | source)
XLA Modules:
  0.0 76.8 jit_solution(8899293857062169353)
XLA Ops:
  0.6 73.5 %attention.1 = (bf16[128,4096]{1,0:T(8,128)(2,1)}, bf16[128,4096]{1,0:T(8,128)(2,1)}, bf16[2,64,512]{2,1,0:T(8,128)(2,1)}, bf16[2,64,512]{2,1,0:T(8,128)(2,1)}) custom-call(s32[64]{0:T(128)} %order_ref.1, s32[8]{0:T(128)} %length_ref.1, bf16[128,4096]{1,0:T(8,128)(2,1)} %q_ref.1, bf16[2,64,512]{2,1,0:T(8,128)(2,1)} %bitcast.4, bf16[2,64,512]{2,1,0:T(8,128)(2,1)} %bitcast.5, ...), custom_call_target="tpu_custom_call" | custom-call | tf_op jit(solution)/shard_map/attention/pallas_call | solution.py:434
  74.1 2.6 %hand_over.1 = (bf16[128,4096]{1,0:T(8,128)(2,1)}, bf16[128,4096]{1,0:T(8,128)(2,1)}, bf16[128,512]{1,0:T(8,128)(2,1)}, bf16[128,512]{1,0:T(8,128)(2,1)}) custom-call(bf16[128,4096]{1,0:T(8,128)(2,1)} %get-tuple-element.8.refs_0_, bf16[128,4096]{1,0:T(8,128)(2,1)} %get-tuple-element.9.refs_1_, bf16[128,512]{1,0:T(8,128)(2,1)} %bitcast.6, ...), custom_call_target="tpu_custom_call" | custom-call | tf_op jit(solution)/shard_map/hand_over/pallas_call | solution.py:456
